TPU v7x, 32 devices: a whole 2x2x4 slice. The times are simulated.
32 devices in a mesh: wide: 8 (over z, y), narrow: 4 (over x, core).
Axes of the slice: x: 2, y: 2, z: 4, core: 2. Of those that a mesh axis runs over, the one named last changes fastest.
Arguments:
- tokens: bfloat16 [64, 512, 768], P(('wide', 'narrow')), may hold values from -18 to 18
- mask_place: int32 [64, 76], P(('wide', 'narrow')), may hold values from 0 to 511, as said below
- mask_count: int32 [64], P(('wide', 'narrow')), may hold values from 38 to 76, as said below
- masked_output_gradient: bfloat16 [64, 76, 768], P(('wide', 'narrow')), may hold values from -6 to 6
- query_key_value_weight: float32 [3, 768, 768], P(None, 'wide'), may hold values from -0.15625 to 0.15625
- qkv_first: float32 [3, 768, 768], P(None, 'wide'), may hold values from -0.00061035156 to 0.00061035156
- qkv_second: float32 [3, 768, 768], P(None, 'wide'), may hold values from 1.4110135e-10 to 5.644054e-10
- out_weight: float32 [768, 768], P(None, 'wide'), may hold values from -1.25 to 1.25
- out_first: float32 [768, 768], P(None, 'wide'), may hold values from -0.00061035156 to 0.00061035156
- out_second: float32 [768, 768], P(None, 'wide'), may hold values from 1.4110135e-10 to 5.644054e-10
- up_weight: float32 [768, 3072], P('wide'), may hold values from -0.21875 to 0.21875
- up_first: float32 [768, 3072], P('wide'), may hold values from -0.00061035156 to 0.00061035156
- up_second: float32 [768, 3072], P('wide'), may hold values from 1.4110135e-10 to 5.644054e-10
- down_weight: float32 [3072, 768], P(None, 'wide'), may hold values from -0.109375 to 0.109375
- down_first: float32 [3072, 768], P(None, 'wide'), may hold values from -0.00061035156 to 0.00061035156
- down_second_moment: float32 [3072, 768], P(None, 'wide'), may hold values from 1.4110135e-10 to 5.644054e-10
- vectors: float32 [8, 768], P(None, 'wide'), may hold values from -1 to 3
- vectors_first: float32 [8, 768], P(None, 'wide'), may hold values from -0.00061035156 to 0.00061035156
- vectors_second: float32 [8, 768], P(None, 'wide'), may hold values from 1.4110135e-10 to 5.644054e-10
- up_bias: float32 [3072], P('wide'), may hold values from -3 to 3
- up_bias_first: float32 [3072], P('wide'), may hold values from -0.00061035156 to 0.00061035156
- up_bias_second: float32 [3072], P('wide'), may hold values from 1.4110135e-10 to 5.644054e-10
Outputs:
- layer_out: bfloat16 [64, 512, 768], P(('wide', 'narrow'))
- tokens_grad: float32 [64, 512, 768], P(('wide', 'narrow'))
- grad_norm: float32 [], replicated
- qkv_new: float32 [3, 768, 768], P(None, 'wide')
- qkv_first_new: float32 [3, 768, 768], P(None, 'wide')
- qkv_second_new: float32 [3, 768, 768], P(None, 'wide')
- out_new: float32 [768, 768], P(None, 'wide')
- out_first_new: float32 [768, 768], P(None, 'wide')
- out_second_new: float32 [768, 768], P(None, 'wide')
- up_new: float32 [768, 3072], P('wide')
- up_first_new: float32 [768, 3072], P('wide')
- up_second_new: float32 [768, 3072], P('wide')
- down_new: float32 [3072, 768], P(None, 'wide')
- down_first_new: float32 [3072, 768], P(None, 'wide')
- down_second_new: float32 [3072, 768], P(None, 'wide')
- updated_gain_vectors: float32 [8, 768], P(None, 'wide')
- vectors_first_new: float32 [8, 768], P(None, 'wide')
- vectors_second_new: float32 [8, 768], P(None, 'wide')
- up_bias_new: float32 [3072], P('wide')
- up_bias_first_new: float32 [3072], P('wide')
- up_bias_second_new: float32 [3072], P('wide')
Inputs may be any that keep to these rules, and one draw needn't show every extreme that they name: `mask_place`: the positions of one row are distinct; slots at and past the row's count are padding and carry no gradient. `mask_count`: some sequence uses all 76 slots.
All inputs are finite; a program needn't handle non-finite values.
Results may differ from a plain program's by a relative error of at most 0.02.
Values may be sent and summed in bfloat16 or wider, within the bound.
A program may use at most 256 MiB of HBM per device.

v0:
```python
import functools

import jax
import jax.numpy as jnp
from jax import lax
from jax.experimental import pallas as pl
from jax.experimental.pallas import tpu as pltpu
from jax.sharding import PartitionSpec as P

HEADS = 12
HEAD_DIM = 64
STEP = 10

LN_EPS = 1e-06
SQRT_HALF = 0.7071067811865476
INV_ROOT_TWO_PI = 0.3989422804014327
CLIP_LIMIT = 1.0
BETA_ONE = 0.9
BETA_TWO = 0.999
LEARN_RATE = 0.05
OUTPUT_RATE = 0.2
VECTOR_RATE = 0.5
BIAS_RATE = 0.3
DECAY_RATE = 0.01
ADAM_EPS = 1e-08

MESH = pl.DeviceIdType.MESH


def when(cond, body):
    if callable(cond):
        cond = cond()
    if cond is None:
        body()
    else:
        pl.when(cond)(body)


class Sends:
    def __init__(self):
        self.started = []

    def start(self, cond, make):
        when(cond, lambda: make().start())
        self.started.append((cond, make))

    def finish(self):
        for cond, make in self.started:
            when(cond, lambda make=make: make().wait_send())


def both(a, b):
    return b if a is None else (a if b is None else jnp.logical_and(a, b))


def place():
    w, n = lax.axis_index("wide"), lax.axis_index("narrow")
    return w // 2, lax.rem(w, 2), n // 2, lax.rem(n, 2)


def flip(v):
    return 1 - v


def dev(z, y, x, c):
    return (z * 2 + y, x * 2 + c)


def meet(z, y, x, c, diagonal):
    bar = pltpu.get_barrier_semaphore()
    peers = [(None, dev(z, flip(y), x, c)), (None, dev(z, y, flip(x), c)), (None, dev(z, y, x, flip(c)))]
    if diagonal:
        peers.append((None, dev(z, y, flip(x), flip(c))))
    peers += [(z > 0, dev(z - 1, y, x, c)), (z < 3, dev(z + 1, y, x, c))]
    for cond, peer in peers:
        when(cond, lambda peer=peer: pl.semaphore_signal(bar, inc=1, device_id=peer, device_id_type=MESH))
    inner = jnp.logical_and(z > 0, z < 3)
    count = 4 if diagonal else 3
    pl.semaphore_wait(bar, count + 1 + jnp.where(inner, 1, 0))


def gather_kernel(rows, cols, attn, up, down, small, attn_full, up_full, down_full, small_full, send_sem, recv_sem, small_send, small_recv, own_sem):
    z, y, x, c = place()
    edge = x == c
    third = cols // 3
    mine, across = x + c, 2 * flip(x)
    fulls = (attn_full, up_full, down_full)
    shards = (attn, up, down)
    sends = Sends()
    zl, zh = z > 0, z < 3

    def spot(p, zz, yy, t):
        return fulls[p].at[pl.ds(pl.multiple_of((zz * 2 + yy) * rows, rows), rows), pl.ds(pl.multiple_of(t * third, third), third)]

    def push(cond, p, zz, yy, t, kind, to, src=None):
        def make():
            w = zz * 2 + yy
            where = spot(p, zz, yy, t)
            return pltpu.make_async_remote_copy(
                src_ref=where if src is None else src,
                dst_ref=where,
                send_sem=send_sem.at[kind, p, w],
                recv_sem=recv_sem.at[p, w, t],
                device_id=to,
                device_id_type=MESH,
            )

        sends.start(cond, make)

    def small_push(cond, zz, yy, kind, to, src=None):
        def make():
            w = zz * 2 + yy
            where = small_full.at[w]
            return pltpu.make_async_remote_copy(
                src_ref=where if src is None else src,
                dst_ref=where,
                send_sem=small_send.at[kind, w],
                recv_sem=small_recv.at[w],
                device_id=to,
                device_id_type=MESH,
            )

        sends.start(cond, make)

    def arrive(cond, p, zz, yy, t):
        def body():
            where = spot(p, zz, yy, t)
            w = zz * 2 + yy
            pltpu.make_async_remote_copy(where, where, send_sem.at[0, p, w], recv_sem.at[p, w, t], dev(z, y, x, c), device_id_type=MESH).wait_recv()

        when(cond, body)

    def small_arrive(cond, zz, yy):
        def body():
            w = zz * 2 + yy
            pltpu.make_async_remote_copy(small_full.at[w], small_full.at[w], small_send.at[0, w], small_recv.at[w], dev(z, y, x, c), device_id_type=MESH).wait_recv()

        when(cond, body)

    UP, DOWN, SIDE, OVER, NEAR, PASS = range(6)
    above, below, beside = dev(z + 1, y, x, c), dev(z - 1, y, x, c), dev(z, flip(y), x, c)
    over, near = dev(z, y, flip(x), c), dev(z, y, x, flip(c))

    def own(p):
        src = shards[p].at[:, pl.ds(pl.multiple_of(mine * third, third), third)]
        push(zh, p, z, y, mine, UP, above, src)
        push(zl, p, z, y, mine, DOWN, below, src)
        push(None, p, z, y, mine, SIDE, beside, src)

    def z_step(p, d):
        for cond, zz, onward, kind, to in ((z - d >= 0, z - d, zh, UP, above), (z + d <= 3, z + d, zl, DOWN, below)):
            arrive(cond, p, zz, y, mine)
            push(both(cond, onward), p, zz, y, mine, kind, to)
            push(cond, p, zz, y, mine, SIDE, beside)
            push(both(cond, edge), p, zz, y, mine, OVER, over)
            push(cond, p, zz, y, mine, NEAR, near)

    def y_step(p, d):
        steps = ((None, z),) if d == 0 else ((z - d >= 0, z - d), (z + d <= 3, z + d))
        for cond, zz in steps:
            arrive(cond, p, zz, flip(y), mine)
            push(both(cond, edge), p, zz, flip(y), mine, OVER, over)
            push(cond, p, zz, flip(y), mine, NEAR, near)

    def x_step(p, d):
        mid = jnp.logical_not(edge)
        for yy in (y, flip(y)):
            if d == 0:
                steps = () if yy is y else ((None, z),)
            else:
                steps = ((z - d >= 0, z - d), (z + d <= 3, z + d))
            for cond, zz in steps:
                cond = both(cond, mid)
                arrive(cond, p, zz, yy, across)
                push(cond, p, zz, yy, across, PASS, near)

    def last(p, d):
        for yy in (y, flip(y)):
            if d == 0:
                steps = () if yy is y else ((None, z),)
            else:
                steps = ((z - d >= 0, z - d), (z + d <= 3, z + d))
            for cond, zz in steps:
                arrive(cond, p, zz, yy, x + flip(c))
                arrive(both(cond, edge), p, zz, yy, across)

    def small_z(d):
        for cond, zz, onward, kind, to in ((z - d >= 0, z - d, zh, UP, above), (z + d <= 3, z + d, zl, DOWN, below)):
            small_arrive(cond, zz, y)
            small_push(both(cond, onward), zz, y, kind, to)
            small_push(cond, zz, y, SIDE, beside)

    meet(z, y, x, c, False)
    small_push(zh, z, y, UP, above, small)
    small_push(zl, z, y, DOWN, below, small)
    small_push(None, z, y, SIDE, beside, small)
    own(0)
    w = z * 2 + y
    copies = []
    for p in range(3):
        copies.append(pltpu.make_async_copy(shards[p], fulls[p].at[pl.ds(pl.multiple_of(w * rows, rows), rows)], own_sem.at[p]))
    copies.append(pltpu.make_async_copy(small, small_full.at[w], own_sem.at[3]))
    for copy in copies:
        copy.start()
    for d in range(1, 4):
        small_z(d)
    order = [
        lambda: z_step(0, 1), lambda: own(1), lambda: y_step(0, 0), lambda: z_step(0, 2), lambda: y_step(0, 1), lambda: x_step(0, 0), lambda: z_step(0, 3),
        lambda: y_step(0, 2), lambda: x_step(0, 1), lambda: z_step(1, 1), lambda: own(2), lambda: y_step(0, 3), lambda: x_step(0, 2), lambda: z_step(1, 2), lambda: y_step(1, 0), lambda: x_step(0, 3), lambda: z_step(1, 3),
        lambda: y_step(1, 1), lambda: x_step(1, 0), lambda: z_step(2, 1), lambda: y_step(1, 2), lambda: x_step(1, 1), lambda: z_step(2, 2), lambda: y_step(1, 3), lambda: x_step(1, 2), lambda: z_step(2, 3),
        lambda: y_step(2, 0), lambda: x_step(1, 3), lambda: y_step(2, 1), lambda: x_step(2, 0), lambda: y_step(2, 2), lambda: x_step(2, 1), lambda: y_step(2, 3), lambda: x_step(2, 2), lambda: x_step(2, 3),
    ]
    for step in order:
        step()
    for d in range(4):
        for cond, zz in (((None, z),) if d == 0 else ((z - d >= 0, z - d), (z + d <= 3, z + d))):
            small_arrive(cond, zz, flip(y))
    for p in range(3):
        for d in range(4):
            last(p, d)
    sends.finish()
    for copy in copies:
        copy.wait()


def gather(attn, up, down, small):
    rows, cols = attn.shape
    full = jax.ShapeDtypeStruct((8 * rows, cols), attn.dtype)
    anywhere = pl.BlockSpec(memory_space=pl.ANY)
    return pl.pallas_call(
        functools.partial(gather_kernel, rows, cols),
        out_shape=(full, full, full, jax.ShapeDtypeStruct((8,) + small.shape, small.dtype)),
        in_specs=[anywhere] * 4,
        out_specs=(anywhere,) * 4,
        scratch_shapes=[
            pltpu.SemaphoreType.DMA((6, 3, 8)),
            pltpu.SemaphoreType.DMA((3, 8, 3)),
            pltpu.SemaphoreType.DMA((3, 8)),
            pltpu.SemaphoreType.DMA((8,)),
            pltpu.SemaphoreType.DMA((4,)),
        ],
        compiler_params=pltpu.CompilerParams(collective_id=0, has_side_effects=True),
    )(attn, up, down, small)


def layer_norm(values, gain, shift):
    center = values - jnp.mean(values, axis=-1, keepdims=True)
    inverse = lax.rsqrt(jnp.mean(center * center, axis=-1, keepdims=True) + LN_EPS)
    normed = center * inverse
    return (normed * gain + shift, normed, inverse)


def norm_back(incoming, normed, inverse, gain):
    dgain = jnp.sum(incoming * normed, axis=0)
    dshift = jnp.sum(incoming, axis=0)
    scaled = incoming * gain
    dvalues = inverse * (
        scaled
        - jnp.mean(scaled, axis=-1, keepdims=True)
        - normed * jnp.mean(scaled * normed, axis=-1, keepdims=True)
    )
    return (dvalues, dgain, dshift)


def mm(a, b, dims, out=jnp.float32):
    return lax.dot_general(a, b, (dims, ((), ())), preferred_element_type=jnp.float32).astype(out)


NN = ((1,), (0,))
NT = ((1,), (1,))
TN = ((0,), (0,))


def split_heads(values, seqs, length):
    return values.reshape(seqs, length, HEADS, HEAD_DIM)


def attend(pieces):
    query, key, value = pieces
    raw = jnp.einsum("qhe,khe->hqk", query, key, preferred_element_type=jnp.float32) * HEAD_DIM ** (
        -0.5
    )
    peak = jnp.max(raw, axis=-1, keepdims=True)
    expo = jnp.exp(raw - peak)
    total = jnp.sum(expo, axis=-1, keepdims=True)
    probs = (expo / total).astype(jnp.bfloat16)
    mixed = jnp.einsum("hqk,khe->qhe", probs, value, preferred_element_type=jnp.float32)
    return mixed.astype(jnp.bfloat16)


def attend_back(pieces):
    query, key, value, dmixed = pieces
    scale = HEAD_DIM ** (-0.5)
    raw = jnp.einsum("qhe,khe->hqk", query, key, preferred_element_type=jnp.float32) * scale
    probs = jax.nn.softmax(raw, axis=-1)
    dprobs = jnp.einsum("qhe,khe->hqk", dmixed, value, preferred_element_type=jnp.float32)
    dscore = probs * (dprobs - jnp.sum(dprobs * probs, axis=-1, keepdims=True))
    dscore = (dscore * scale).astype(jnp.bfloat16)
    dquery = jnp.einsum("hqk,khe->qhe", dscore, key, preferred_element_type=jnp.float32)
    dkey = jnp.einsum("hqk,qhe->khe", dscore, query, preferred_element_type=jnp.float32)
    dvalue = jnp.einsum(
        "hqk,qhe->khe", probs.astype(jnp.bfloat16), dmixed, preferred_element_type=jnp.float32
    )
    return (dquery, dkey, dvalue)


def adam_step(weight, first, second, grad, factor, decay, rate):
    grad = grad * factor
    first_new = BETA_ONE * first + (1.0 - BETA_ONE) * grad
    second_new = BETA_TWO * second + (1.0 - BETA_TWO) * grad * grad
    mean_hat = first_new / (1.0 - BETA_ONE**STEP)
    square_hat = second_new / (1.0 - BETA_TWO**STEP)
    weight_new = weight - rate * (mean_hat / (jnp.sqrt(square_hat) + ADAM_EPS) + decay * weight)
    return (weight_new, first_new, second_new)


def dot(a, b, dims):
    return lax.dot_general(a, b, (dims, ((), ())), preferred_element_type=jnp.float32)


NN = ((1,), (0,))
NT = ((1,), (1,))
TN = ((0,), (0,))
LOW = jnp.bfloat16


def norm(values, gain, shift):
    center = values - jnp.mean(values, axis=-1, keepdims=True)
    inverse = lax.rsqrt(jnp.mean(center * center, axis=-1, keepdims=True) + LN_EPS)
    normed = center * inverse
    return normed * gain + shift, normed, inverse


def norm_pull(incoming, normed, inverse, gain):
    dgain = jnp.sum(incoming * normed, axis=0, keepdims=True)
    dshift = jnp.sum(incoming, axis=0, keepdims=True)
    scaled = incoming * gain
    return (
        inverse * (scaled - jnp.mean(scaled, axis=-1, keepdims=True) - normed * jnp.mean(scaled * normed, axis=-1, keepdims=True)),
        dgain,
        dshift,
    )


def forward_kernel(
    rows, seqs, length, padded,
    attn, up, down, small, tokens, pick, grad,
    attn_o, up_o, down_o, vec_o, bias_o, kv_o, hidden_o, query_o, rows_o, mixed_o, hid_o, act_o, slope_o, dtwo_o, dlow_o, normed_o, inv_o, dvec_o,
    attn_full, up_full, down_full, small_full,
    qkv, mixed, hidden, vec, qbias, bias, query_m, rows_m, mixed_m, hid_m, act_m, slope, ytwo, dtwo, dlow, dvec, hid_f, normed_one, inverse_one,
    send_sem, recv_sem, small_send, small_recv, own_sem, save_sem, pair_send, pair_recv,
):
    z, y, x, c = place()
    width = tokens.shape[1]
    cols = attn.shape[1]
    edge = x == c
    third = cols // 3
    mine, across = x + c, 2 * flip(x)
    fulls = (attn_full, up_full, down_full)
    shards = (attn, up, down)
    sends = Sends()
    zl, zh = z > 0, z < 3
    count = seqs * padded

    def spot(p, zz, yy, t):
        return fulls[p].at[pl.ds(pl.multiple_of((zz * 2 + yy) * rows, rows), rows), pl.ds(pl.multiple_of(t * third, third), third)]

    def push(cond, p, zz, yy, t, kind, to, src=None):
        def make():
            w = zz * 2 + yy
            where = spot(p, zz, yy, t)
            return pltpu.make_async_remote_copy(
                src_ref=where if src is None else src,
                dst_ref=where,
                send_sem=send_sem.at[kind, p, w],
                recv_sem=recv_sem.at[p, w, t],
                device_id=to,
                device_id_type=MESH,
            )

        sends.start(cond, make)

    def small_push(cond, zz, yy, kind, to, src=None):
        def make():
            w = zz * 2 + yy
            where = small_full.at[w]
            return pltpu.make_async_remote_copy(
                src_ref=where if src is None else src,
                dst_ref=where,
                send_sem=small_send.at[kind, w],
                recv_sem=small_recv.at[w],
                device_id=to,
                device_id_type=MESH,
            )

        sends.start(cond, make)

    def arrive(cond, p, zz, yy, t):
        def body():
            where = spot(p, zz, yy, t)
            w = zz * 2 + yy
            pltpu.make_async_remote_copy(where, where, send_sem.at[0, p, w], recv_sem.at[p, w, t], dev(z, y, x, c), device_id_type=MESH).wait_recv()

        when(cond, body)

    def small_arrive(cond, zz, yy):
        def body():
            w = zz * 2 + yy
            pltpu.make_async_remote_copy(small_full.at[w], small_full.at[w], small_send.at[0, w], small_recv.at[w], dev(z, y, x, c), device_id_type=MESH).wait_recv()

        when(cond, body)

    UP, DOWN, SIDE, OVER, NEAR, PASS = range(6)
    above, below, beside = dev(z + 1, y, x, c), dev(z - 1, y, x, c), dev(z, flip(y), x, c)
    over, near = dev(z, y, flip(x), c), dev(z, y, x, flip(c))

    def around(d):
        return ((None, z),) if d == 0 else ((z - d >= 0, z - d), (z + d <= 3, z + d))

    def own(p):
        src = shards[p].at[:, pl.ds(pl.multiple_of(mine * third, third), third)]
        push(zh, p, z, y, mine, UP, above, src)
        push(zl, p, z, y, mine, DOWN, below, src)
        push(None, p, z, y, mine, SIDE, beside, src)

    def z_step(p, d):
        for cond, zz, onward, kind, to in ((z - d >= 0, z - d, zh, UP, above), (z + d <= 3, z + d, zl, DOWN, below)):
            arrive(cond, p, zz, y, mine)
            push(both(cond, onward), p, zz, y, mine, kind, to)
            push(cond, p, zz, y, mine, SIDE, beside)
            push(both(cond, edge), p, zz, y, mine, OVER, over)
            push(cond, p, zz, y, mine, NEAR, near)

    def y_step(p, d):
        for cond, zz in around(d):
            arrive(cond, p, zz, flip(y), mine)
            push(both(cond, edge), p, zz, flip(y), mine, OVER, over)
            push(cond, p, zz, flip(y), mine, NEAR, near)

    def x_step(p, d):
        mid = jnp.logical_not(edge)
        for yy in (y, flip(y)):
            for cond, zz in () if d == 0 and yy is y else around(d):
                cond = both(cond, mid)
                arrive(cond, p, zz, yy, across)
                push(cond, p, zz, yy, across, PASS, near)

    def last(p):
        for d in range(4):
            for yy in (y, flip(y)):
                for cond, zz in () if d == 0 and yy is y else around(d):
                    arrive(cond, p, zz, yy, x + flip(c))
                    arrive(both(cond, edge), p, zz, yy, across)
        copies[p].wait()
        keep(fulls[p], (attn_o, up_o, down_o)[p], p)

    def small_z(d):
        for cond, zz, onward, kind, to in ((z - d >= 0, z - d, zh, UP, above), (z + d <= 3, z + d, zl, DOWN, below)):
            small_arrive(cond, zz, y)
            small_push(both(cond, onward), zz, y, kind, to)
            small_push(cond, zz, y, SIDE, beside)

    saves = []

    def keep(src, dst, k):
        copy = pltpu.make_async_copy(src, dst, save_sem.at[k])
        copy.start()
        saves.append(copy)

    swaps = []

    def swap(ref, k):
        def make():
            return pltpu.make_async_remote_copy(ref.at[0], ref.at[1], pair_send.at[k], pair_recv.at[k], near, device_id_type=MESH)

        make().start()
        swaps.append((make, ref))

    def vectors():
        for d in range(4):
            for cond, zz in around(d):
                small_arrive(cond, zz, flip(y))
        copies[3].wait()
        at = lax.broadcasted_iota(jnp.int32, (128, width), 0)
        to = lax.broadcasted_iota(jnp.int32, (128, width), 1)
        total = jnp.zeros((16, width), jnp.float32)
        for w in range(8):
            place_w = jnp.logical_and(at + w * rows == to, at < rows).astype(jnp.float32).astype(LOW)
            total += dot(small_full[w], place_w, NN)
            for r in range(3):
                bias[:, pl.ds(w * 384 + r * 128, 128)] = small_full[w, 8 + r : 9 + r, :].astype(jnp.float32)
        vec[...] = total[:8]
        qbias[0] = total[0:1]
        qbias[1] = jnp.zeros((1, width), jnp.float32)
        qbias[2] = total[1:2]

    def project(i):
        r = pl.ds(i * 256, 256)

        @pl.loop(0, 3)
        def _(k):
            value = dot(tokens[r, :], attn_full[:, pl.ds(pl.multiple_of(k * width, width), width)], NN) + qbias[k]
            qkv[k, r, :] = (value * jnp.where(k == 0, 0.125, 1.0)).astype(LOW)

    def attend(s, j):
        lane = lax.broadcasted_iota(jnp.int32, (length, 128), 1) < 64
        cs = pl.ds(j * 128, 128)
        rs = pl.ds(s * length, length)
        key, value = qkv[1, rs, cs], qkv[2, rs, cs]
        zero, one = jnp.zeros_like(key), jnp.ones_like(key)
        keys = (jnp.where(lane, key, zero), jnp.where(lane, zero, key))
        values = (jnp.where(lane, value, one), jnp.where(lane, one, value))
        for q in range(length // 256):
            r = pl.ds(s * length + q * 256, 256)
            query = qkv[0, r, cs]
            parts = []
            for h in range(2):
                score = dot(query, keys[h], NT)
                expo = jnp.exp(score - jnp.max(score, axis=-1, keepdims=True))
                parts.append(dot(expo.astype(LOW), values[h], NN))
            left = lane[:256]
            top = jnp.where(left, parts[0], parts[1])
            under = pltpu.roll(jnp.where(left, parts[1], parts[0]), 64, 1)
            mixed[r, cs] = (top / under).astype(LOW)

    def middle(i):
        r = pl.ds(i * 256, 256)
        pre = tokens[r, :].astype(jnp.float32) + (dot(mixed[r, :], attn_full[:, pl.ds(3 * width, width)], NT) + vec[2:3, :])
        hidden[r, :] = norm(pre, vec[3:4, :], vec[4:5, :])[0]

    def masked_rows():
        for s in range(seqs):
            r = pl.ds(s * padded, padded)
            rs = pl.ds(s * length, length)
            rows_m[0, r, :] = dot(pick[s], tokens[rs, :], NN).astype(LOW)
            mixed_m[0, r, :] = dot(pick[s], mixed[rs, :], NN).astype(LOW)
            query_m[r, :] = dot(pick[s], qkv[0, rs, :], NN).astype(LOW)
        pre = rows_m[0].astype(jnp.float32) + (dot(mixed_m[0], attn_full[:, pl.ds(3 * width, width)], NT) + vec[2:3, :])
        value, normed, inverse = norm(pre, vec[3:4, :], vec[4:5, :])
        hid_f[...] = value
        hid_m[0] = value.astype(LOW)
        normed_one[...] = normed
        inverse_one[...] = jnp.broadcast_to(inverse, inverse_one.shape)
        swap(rows_m, 0)
        swap(mixed_m, 1)
        swap(hid_m, 2)
        keep(query_m, query_o, 3)
        keep(normed_one, normed_o, 4)
        keep(inverse_one, inv_o, 5)

    def upper(k):
        f = pl.ds(k * 768, 768)
        u = dot(hid_m[0], up_full[:, f], NN) + bias[:, f]
        cumul = 0.5 * (1.0 + lax.erf(u * SQRT_HALF))
        act_m[0, :, f] = (u * cumul).astype(LOW)
        slope[:, f] = cumul + u * (jnp.exp(-0.5 * u * u) * INV_ROOT_TWO_PI)

    def after_upper():
        swap(act_m, 3)
        keep(slope, slope_o, 6)

    def lower():
        @pl.loop(0, 3)
        def _(k):
            n = pl.ds(pl.multiple_of(k * 256, 256), 256)
            ytwo[:, n] = dot(act_m[0], down_full[n, :], NT)

        pre = hid_f[...] + (ytwo[...] + vec[5:6, :])
        _, normed, inverse = norm(pre, vec[6:7, :], vec[7:8, :])
        value, dgain, dshift = norm_pull(grad[...].astype(jnp.float32), normed, inverse, vec[6:7, :])
        dtwo[...] = value
        dlow[0] = value.astype(LOW)
        dvec[...] = jnp.zeros_like(dvec)
        dvec[5:6, :] = jnp.sum(value, axis=0, keepdims=True)
        dvec[6:7, :] = dgain
        dvec[7:8, :] = dshift
        swap(dlow, 4)
        keep(dtwo, dtwo_o, 7)
        keep(dvec, dvec_o, 8)

    meet(z, y, x, c, False)
    small_push(zh, z, y, UP, above, small)
    small_push(zl, z, y, DOWN, below, small)
    small_push(None, z, y, SIDE, beside, small)
    own(0)
    w = z * 2 + y
    copies = []
    for p in range(3):
        copies.append(pltpu.make_async_copy(shards[p], fulls[p].at[pl.ds(pl.multiple_of(w * rows, rows), rows)], own_sem.at[p]))
    copies.append(pltpu.make_async_copy(small, small_full.at[w], own_sem.at[3]))
    for copy in copies:
        copy.start()
    for d in range(1, 4):
        small_z(d)

    def save_hidden():
        keep(hidden, hidden_o, 9)
        keep(qkv.at[pl.ds(1, 2)], kv_o, 10)

    head = [
        lambda: z_step(0, 1), lambda: own(1), lambda: y_step(0, 0), lambda: z_step(0, 2), lambda: y_step(0, 1), lambda: x_step(0, 0), lambda: z_step(0, 3),
        lambda: y_step(0, 2), lambda: x_step(0, 1), vectors, lambda: z_step(1, 1), lambda: own(2), lambda: y_step(0, 3), lambda: x_step(0, 2), lambda: z_step(1, 2), lambda: y_step(1, 0), lambda: x_step(0, 3), lambda: z_step(1, 3),
        lambda: last(0),
    ]
    links = [
        lambda: y_step(1, 1), lambda: x_step(1, 0), lambda: z_step(2, 1), lambda: y_step(1, 2), lambda: x_step(1, 1), lambda: z_step(2, 2), lambda: y_step(1, 3), lambda: x_step(1, 2), lambda: z_step(2, 3),
        lambda: y_step(2, 0), lambda: x_step(1, 3), lambda: y_step(2, 1), lambda: x_step(2, 0), lambda: y_step(2, 2),
    ]
    work = [functools.partial(project, i) for i in range(4)]
    work += [functools.partial(attend, s, j) for s in range(seqs) for j in range(width // 128)]
    work += [functools.partial(middle, i) for i in range(4)]
    work += [masked_rows]
    for step in head:
        step()
    done = 0
    for k, step in enumerate(links):
        upto = len(work) * (k + 1) // len(links)
        for piece in work[done:upto]:
            piece()
        done = upto
        step()
    save_hidden()
    last(1)
    for k in range(4):
        upper(k)
        (lambda: x_step(2, 1), lambda: y_step(2, 3), lambda: x_step(2, 2), lambda: x_step(2, 3))[k]()
    after_upper()
    last(2)
    lower()
    keep(vec, vec_o, 11)
    keep(bias, bias_o, 12)
    for make, ref in swaps:
        make().wait_recv()
    for k, (ref, dst) in enumerate(((rows_m, rows_o), (mixed_m, mixed_o), (hid_m, hid_o), (act_m, act_o), (dlow, dlow_o))):
        keep(ref, dst, 13 + k)
    for make, ref in swaps:
        make().wait_send()
    sends.finish()
    for copy in saves:
        copy.wait()


def forward(attn, up, down, small, tokens, pick, grad):
    rows, cols = attn.shape
    width = tokens.shape[1]
    seqs, padded, length = pick.shape
    total = tokens.shape[0]
    count = seqs * padded
    shape = jax.ShapeDtypeStruct
    f = jnp.float32
    full = shape((8 * rows, cols), LOW)
    anywhere = pl.BlockSpec(memory_space=pl.ANY)
    vm = pl.BlockSpec(memory_space=pltpu.VMEM)
    dma = pltpu.SemaphoreType.DMA
    outs = (
        full, full, full, shape((8, width), f), shape((1, cols), f), shape((2, total, width), LOW), shape((total, width), f),
        shape((count, width), LOW), shape((2, count, width), LOW), shape((2, count, width), LOW), shape((2, count, width), LOW),
        shape((2, count, cols), LOW), shape((count, cols), f), shape((count, width), f), shape((2, count, width), LOW),
        shape((count, width), f), shape((count, 128), f), shape((8, width), f),
    )
    v = pltpu.VMEM
    return pl.pallas_call(
        functools.partial(forward_kernel, rows, seqs, length, padded),
        out_shape=outs,
        in_specs=[anywhere] * 4 + [vm] * 3,
        out_specs=(anywhere,) * len(outs),
        scratch_shapes=[
            v((8 * rows, cols), LOW), v((8 * rows, cols), LOW), v((8 * rows, cols), LOW), v((8, 16, 128), LOW),
            v((3, total, width), LOW), v((total, width), LOW), v((total, width), f), v((8, width), f), v((3, 1, width), f), v((1, cols), f),
            v((count, width), LOW), v((2, count, width), LOW), v((2, count, width), LOW), v((2, count, width), LOW), v((2, count, cols), LOW),
            v((count, cols), f), v((count, width), f), v((count, width), f), v((2, count, width), LOW), v((8, width), f),
            v((count, width), f), v((count, width), f), v((count, 128), f),
            dma((6, 3, 8)), dma((3, 8, 3)), dma((3, 8)), dma((8,)), dma((4,)), dma((18,)), dma((5,)), dma((5,)),
        ],
        compiler_params=pltpu.CompilerParams(collective_id=0, has_side_effects=True, vmem_limit_bytes=60 * 2**20),
    )(attn, up, down, small, tokens, pick, grad)


E = 768
M = 1536
SLAB = 32
ORDER = (3, 0, 2, 1)


def slabs(rows, body):
    @pl.loop(0, rows // SLAB)
    def _(i):
        body(pl.multiple_of(i * SLAB, SLAB))


def f32(v):
    return v.astype(jnp.float32)


def backward_kernel(
    rows, seqs, length, padded,
    attn_h, up_h, down_h, vec, bias, kv_h, hidden_h, query_h, rows_h, mixed_h, hid_h, act_h, slope_h, dtwo_h, dlow_h, normed_h, inv_h, dvec_h, tokens_h, spots,
    layer_h, dtokens_h, out, small_out, norm_out,
    attn, up, down, kv, query_m, rows_m, mixed_m, hid_m, act_m, slope, dtwo, dlow, normed, inverse, dvec, tokens,
    left, right, dupper, dbias, dhid, dpre, done, dmix, dquery, dkv, part, tokens_t,
    htile, ytile, ltile,
    acc, xb, yr, zr, mr,
    sall, sall2, ssib, sx, sy, szu, szd, norms,
    load_sem, tile_sem, out_sem, pair_s, pair_r, dup_s, dup_r, sib_s, sib_r, x_s, x_r, y_s, y_r, z_s, z_r, m_s, m_r, f_s, f_r, sm_s, sm_r, n_s, n_r,
):
    z, y, x, c = place()
    edge = x == c
    mid = jnp.logical_not(edge)
    width = E
    count = seqs * padded
    total = seqs * length
    pair = rows * 2
    sends = Sends()
    me = dev(z, y, x, c)
    above, below, beside = dev(z + 1, y, x, c), dev(z - 1, y, x, c), dev(z, flip(y), x, c)
    over, near, diag = dev(z, y, flip(x), c), dev(z, y, x, flip(c)), dev(z, y, flip(x), flip(c))
    ecol = pl.multiple_of(x * 2304, 768)
    ocol = pl.multiple_of(flip(x) * 2304, 768)

    loads = []
    for k, (src, dst) in enumerate((
        (dlow_h, dlow), (act_h, act_m), (down_h, down), (slope_h, slope), (hid_h, hid_m), (up_h, up), (dtwo_h, dtwo), (normed_h, normed),
        (inv_h, inverse), (dvec_h, dvec), (attn_h, attn), (mixed_h, mixed_m), (query_h, query_m), (kv_h, kv), (rows_h, rows_m), (tokens_h, tokens),
    )):
        loads.append(pltpu.make_async_copy(src, dst, load_sem.at[k]))
        loads[-1].start()
    (L_DLOW, L_ACT, L_DOWN, L_SLOPE, L_HID, L_UP, L_DTWO, L_NORMED, L_INV, L_DVEC, L_ATTN, L_MIXED, L_QUERY, L_KV, L_ROWS, L_TOKENS) = range(16)

    def need(*ks):
        for k in ks:
            loads[k].wait()

    def copy(src, dst, ss, rs, to):
        return pltpu.make_async_remote_copy(src_ref=src, dst_ref=dst, send_sem=ss, recv_sem=rs, device_id=to, device_id_type=MESH)

    def wait(cond, dst, rs):
        when(cond, lambda: copy(dst, dst, rs, rs, me).wait_recv())

    def zrows(zz):
        return pl.ds(zz * pair, pair)

    def wrows(zz, yy):
        return pl.ds(pl.multiple_of((zz * 2 + yy) * rows, rows), rows)

    def add_x(p, zz):
        @pl.when(edge)
        def _():
            wait(None, xb.at[p, zrows(zz)], x_r.at[p, zz])

            def one(i):
                r = pl.ds(zz * pair + i, SLAB)
                acc[p, r, pl.ds(0, E)] = (f32(acc[p, r, pl.ds(0, E)]) + f32(xb[p, r, :])).astype(LOW)

            slabs(pair, one)

        push_y(edge, p, zz, E)

    def push_x(p, zz):
        sends.start(mid, lambda: copy(xb.at[p, zrows(zz)], xb.at[p, zrows(zz)], x_s.at[p, zz], x_r.at[p, zz], over))

    def push_y(cond, p, zz, wide):
        sends.start(cond, lambda: copy(
            acc.at[p, wrows(zz, flip(y)), pl.ds(0, wide)], yr.at[p, zz, :, pl.ds(0, wide)], y_s.at[p, zz], y_r.at[p, zz], beside))

    def add_into(cond, p, zz, buffer, slot, sem):
        for role, wide in ((edge, E), (mid, M)):
            @pl.when(both(cond, role))
            def _():
                wait(None, buffer.at[p, slot, :, pl.ds(0, wide)], sem)
                base = (zz * 2 + y) * rows

                def one(i):
                    here = pl.ds(pl.multiple_of(base + i, SLAB), SLAB)
                    acc[p, here, pl.ds(0, wide)] = (f32(acc[p, here, pl.ds(0, wide)]) + f32(buffer[p, slot, pl.ds(i, SLAB), pl.ds(0, wide)])).astype(LOW)

                slabs(rows, one)

    def add_y(p, zz):
        add_into(None, p, zz, yr, zz, y_r.at[p, zz])

    def z_push(cond, p, spot, k, to):
        for role, wide in ((edge, E), (mid, M)):
            def make(wide=wide):
                zz, slot = spot()
                return copy(acc.at[p, wrows(zz, y), pl.ds(0, wide)], zr.at[p, slot, :, pl.ds(0, wide)], z_s.at[k, p, zz], z_r.at[k, p, zz], to)

            sends.start(lambda role=role: both(cond(), role), make)

    def line(p, t):
        def upward():
            return both(z <= t, z < 3)

        def up_spot():
            zz = jnp.where(upward(), 3 + z - t, 0)
            return zz, zz

        def downward():
            return both(3 - z <= t, z > 0)

        def down_spot():
            zz = jnp.where(downward(), z + t - 3, 0)
            return zz, jnp.where(zz == z - 1, 4, zz)

        zz = up_spot()[0]
        add_into(both(upward(), z > 0), p, zz, zr, zz, z_r.at[0, p, zz])
        z_push(upward, p, up_spot, 0, above)
        zz = down_spot()[0]
        add_into(both(downward(), z < 3), p, zz, zr, zz, z_r.at[1, p, zz])
        z_push(downward, p, down_spot, 1, below)

    def owner(p):
        add_into(z > 0, p, z, zr, z, z_r.at[0, p, z])
        add_into(z < 3, p, z, zr, 4, z_r.at[1, p, z])
        sends.start(mid, lambda: copy(acc.at[p, wrows(z, y)], mr.at[p], m_s.at[p], m_r.at[p], diag))
        base = (z * 2 + y) * rows

        @pl.when(edge)
        def _():
            def one(i):
                out[p, pl.ds(i, SLAB), pl.ds(ecol, E)] = acc[p, pl.ds(pl.multiple_of(base + i, SLAB), SLAB), pl.ds(0, E)]

            slabs(rows, one)

        for k, to in enumerate((near, over, diag)):
            sends.start(edge, lambda k=k, to=to: copy(
                out.at[p, :, pl.ds(ecol, E)], out.at[p, :, pl.ds(ecol, E)], f_s.at[p, k], f_r.at[p, x], to))

    def middle_x(p):
        base = (z * 2 + y) * rows

        @pl.when(mid)
        def _():
            wait(None, mr.at[p], m_r.at[p])

            def one(i):
                out[p, pl.ds(i, SLAB), pl.ds(E, M)] = (f32(acc[p, pl.ds(pl.multiple_of(base + i, SLAB), SLAB), :]) + f32(mr[p, pl.ds(i, SLAB), :])).astype(LOW)

            slabs(rows, one)

        sends.start(mid, lambda: copy(out.at[p, :, pl.ds(E, M)], out.at[p, :, pl.ds(E, M)], f_s.at[p, 0], f_r.at[p, 2], near))

    def arrived(p):
        for xx in range(2):
            wait(jnp.logical_not(both(edge, x == xx)), out.at[p, :, pl.ds(2304 * xx, E)], f_r.at[p, xx])
        wait(edge, out.at[p, :, pl.ds(E, M)], f_r.at[p, 2])

    swaps = []

    def swap(ref, k):
        def make():
            return copy(ref.at[0], ref.at[1], pair_s.at[k], pair_r.at[k], near)

        make().start()
        swaps.append(make)

    def transpose_into(ref):
        for k in range(2):
            left[k] = ref[k].T

    def product(zz, ref, cols):
        return (dot(left[0, zrows(zz), :], ref[0, :, cols], NN) + dot(left[1, zrows(zz), :], ref[1, :, cols], NN)).astype(LOW)

    def grads(p, zz, ref):
        @pl.when(mid)
        def _():
            xb[p, zrows(zz), :] = product(zz, ref, pl.ds(ocol, E))

        push_x(p, zz)

        @pl.when(mid)
        def _():
            for k in range(2):
                acc[p, zrows(zz), pl.ds(k * E, E)] = product(zz, ref, pl.ds(E + k * E, E))

        push_y(mid, p, zz, M)

        @pl.when(edge)
        def _():
            acc[p, zrows(zz), pl.ds(0, E)] = product(zz, ref, pl.ds(ecol, E))

    def dup_copy(k):
        f = pl.ds(k * 768, 768)
        return copy(dupper.at[0, :, f], dupper.at[1, :, f], dup_s.at[k], dup_r.at[k], near)

    def upper_back(k):
        f = pl.ds(k * 768, 768)
        value = dot(dlow[0], down[:, f], NN) * slope[:, f]
        dbias[:, f] = jnp.sum(value, axis=0, keepdims=True)
        dupper[0, :, f] = value.astype(LOW)
        dup_copy(k).start()

    def hidden_back():
        @pl.loop(0, 3)
        def _(k):
            n = pl.ds(pl.multiple_of(k * 256, 256), 256)
            dhid[:, n] = dot(dupper[0], up[n, :], NT)

        value, dgain, dshift = norm_pull(dtwo[...] + dhid[...], normed[...], inverse[:, :1], vec[3:4, :])
        dpre[...] = value
        done[0] = value.astype(LOW)
        swap(done, 0)
        dvec[2:3, :] = jnp.sum(value, axis=0, keepdims=True)
        dvec[3:4, :] = dgain
        dvec[4:5, :] = dshift
        dmix[...] = dot(done[0], attn[:, pl.ds(3 * width, width)], NN).astype(LOW)

    def attend_back(step):
        s, j = step // 6, lax.rem(step, 6)
        cs = pl.ds(pl.multiple_of(j * 128, 128), 128)
        rs = pl.ds(pl.multiple_of(s * length, length), length)
        ms = pl.ds(pl.multiple_of(s * padded, padded), padded)
        lane = lax.broadcasted_iota(jnp.int32, (padded, 128), 1) < 64

        def halves(v):
            zero = jnp.zeros_like(v)
            return jnp.concatenate([jnp.where(lane, v, zero), jnp.where(lane, zero, v)], axis=0)

        key, value = kv[0, rs, cs], kv[1, rs, cs]
        queries, mixes = halves(query_m[ms, cs]), halves(dmix[ms, cs])
        score = dot(key, queries, NT)
        expo = jnp.exp(score - jnp.max(score, axis=0, keepdims=True))
        probs = expo / jnp.sum(expo, axis=0, keepdims=True)
        dprobs = dot(value, mixes, NT)
        dscore = (probs * (dprobs - jnp.sum(dprobs * probs, axis=0, keepdims=True))).astype(LOW)
        dkv[0, rs, cs] = dot(dscore, queries, NN).astype(LOW)
        dvalue = dot(probs.astype(LOW), mixes, NN)
        dkv[1, rs, cs] = dvalue.astype(LOW)
        dq = dot(dscore, key, TN) * 0.125
        dq = jnp.where(lane, dq[:padded], dq[padded:])
        dquery[0, ms, cs] = dq.astype(LOW)
        first = s == 0
        sums = jnp.concatenate([jnp.sum(dq, axis=0, keepdims=True), jnp.sum(dvalue, axis=0, keepdims=True)], axis=0)
        dvec[0:2, cs] = sums + jnp.where(first, 0.0, dvec[0:2, cs])

    def key_value_grads():
        for i in range(total // 256):
            r = pl.ds(i * 256, 256)
            tokens_t[:, r] = tokens[r, :].T

        def fill(store):
            @pl.loop(0, 8)
            def _(i):
                k = lax.rem(i, 2)
                n = pl.ds(pl.multiple_of(i // 2 * pair, pair), pair)
                store(n, pl.ds(pl.multiple_of(k * E, E), E), dot(tokens_t[n, :], dkv[k], NN).astype(LOW))

        @pl.when(mid)
        def _():
            def store(n, cols, value):
                acc[2, n, cols] = value

            fill(store)

        @pl.when(edge)
        def _():
            def store(n, cols, value):
                part[n, cols] = value

            fill(store)

        for zz in ORDER:
            sends.start(edge, lambda zz=zz: copy(part.at[zrows(zz)], part.at[zrows(zz)], sib_s.at[zz], sib_r.at[zz], near))

    def attention_sides():
        for k in range(2):
            left[k] = jnp.where(c == 0, rows_m[k], done[k]).T
            right[k] = jnp.where(c == 0, dquery[k], mixed_m[k])

    def attention_grads(zz):
        @pl.when(mid)
        def _():
            xb[2, zrows(zz), :] = product(zz, right, pl.ds(0, E))

        push_x(2, zz)

        @pl.when(mid)
        def _():
            wait(None, part.at[zrows(zz)], sib_r.at[zz])

            def one(i):
                r = pl.ds(zz * pair + i, SLAB)
                acc[2, r, :] = (f32(acc[2, r, :]) + f32(part[r, :])).astype(LOW)

            slabs(pair, one)

        push_y(mid, 2, zz, M)

        @pl.when(edge)
        def _():
            acc[2, zrows(zz), pl.ds(0, E)] = product(zz, right, pl.ds(0, E))

    def tile_load(i):
        slot = lax.rem(i, 2)
        return pltpu.make_async_copy(hidden_h.at[pl.ds(pl.multiple_of(i * 256, 256), 256)], htile.at[slot], tile_sem.at[slot])

    def layer_store(i):
        slot = lax.rem(i, 2)
        return pltpu.make_async_copy(ltile.at[slot], layer_h.at[pl.ds(pl.multiple_of(i * 256, 256), 256)], out_sem.at[slot])

    def feed_forward(step):
        i, k = step // 4, lax.rem(step, 4)
        slot = lax.rem(i, 2)

        @pl.when(k == 0)
        def _():
            tile_load(i).wait()

            @pl.when(i + 1 < total // 256)
            def _():
                tile_load(i + 1).start()

        f = pl.ds(pl.multiple_of(k * 768, 768), 768)
        u = dot(htile[slot].astype(LOW), up[:, f], NN) + bias[:, f]
        a = (u * (0.5 * (1.0 + lax.erf(u * SQRT_HALF)))).astype(LOW)
        ytile[...] = dot(a, down[:, f], NT) + jnp.where(k == 0, htile[slot] + vec[5:6, :], ytile[...])

        @pl.when(k == 3)
        def _():
            @pl.when(i >= 2)
            def _():
                layer_store(i - 2).wait()

            ltile[slot] = norm(ytile[...], vec[6:7, :], vec[7:8, :])[0].astype(LOW)
            layer_store(i).start()

    def token_store(i):
        slot = lax.rem(i, 2)
        return pltpu.make_async_copy(htile.at[slot], dtokens_h.at[pl.ds(pl.multiple_of(i * 256, 256), 256)], out_sem.at[2 + slot])

    def masked_tokens():
        dpre[...] = dpre[...] + dot(dquery[0], attn[:, pl.ds(0, width)], NT)

    def tokens_back(i):
        slot = lax.rem(i, 2)

        @pl.when(i >= 2)
        def _():
            token_store(i - 2).wait()

        r = pl.ds(pl.multiple_of(i * 256, 256), 256)
        s = i // (length // 256)
        here = lax.broadcasted_iota(jnp.int32, (256, padded), 0) + lax.rem(i, length // 256) * 256
        pick = (here == spots[pl.ds(s, 1), :]).astype(jnp.float32).astype(LOW)
        value = dpre[pl.ds(pl.multiple_of(s * padded, padded), padded), :]
        high = value.astype(LOW)
        rest = (value - f32(high)).astype(LOW)
        htile[slot] = (
            dot(dkv[0, r, :], attn[:, pl.ds(width, width)], NT) + dot(dkv[1, r, :], attn[:, pl.ds(2 * width, width)], NT) + (dot(pick, high, NN) + dot(pick, rest, NN))
        )
        token_store(i).start()

    def small_start():
        for w in range(8):
            sall[w] = jnp.zeros((16, 128), jnp.float32)
            turned = dvec[...] if w == 0 else pltpu.roll(dvec[...], width - rows * w, 1)
            lane = lax.broadcasted_iota(jnp.int32, (8, 128), 1)
            sall[w, 0:8, :] = jnp.where(lane < rows, turned[:, :128], 0.0)
            for r in range(3):
                sall[w, 8 + r : 9 + r, :] = dbias[:, pl.ds(w * 384 + r * 128, 128)]
        sends.start(None, lambda: copy(sall, ssib, sm_s.at[0], sm_r.at[0], near))

    def small_x():
        wait(None, ssib, sm_r.at[0])
        ssib[...] = sall[...] + ssib[...]
        sends.start(None, lambda: copy(ssib, sx, sm_s.at[1], sm_r.at[1], over))

    def small_y():
        wait(None, sx, sm_r.at[1])
        sall2[...] = ssib[...] + sx[...]
        for zz in range(4):
            sends.start(None, lambda zz=zz: copy(sall2.at[zz * 2 + flip(y)], sy.at[zz], sm_s.at[2 + zz], sm_r.at[2 + zz], beside))

    def small_add():
        for zz in range(4):
            wait(None, sy.at[zz], sm_r.at[2 + zz])
            sy[zz] = sy[zz] + sall2[zz * 2 + y]

    def small_line():
        for zz in ORDER:
            @pl.when(both(z <= zz, z > 0))
            def _():
                wait(None, szu.at[zz], sm_r.at[6 + zz])
                sy[zz] = sy[zz] + szu[zz]

            sends.start(lambda zz=zz: z < zz, lambda zz=zz: copy(sy.at[zz], szu.at[zz], sm_s.at[6 + zz], sm_r.at[6 + zz], above))

            @pl.when(both(z >= zz, z < 3))
            def _():
                wait(None, szd.at[zz], sm_r.at[10 + zz])
                sy[zz] = sy[zz] + szd[zz]

            sends.start(lambda zz=zz: z > zz, lambda zz=zz: copy(sy.at[zz], szd.at[zz], sm_s.at[10 + zz], sm_r.at[10 + zz], below))

    w = z * 2 + y

    def peer(k):
        return lax.rem(w + k, 8)

    def square_sum():
        small_out[...] = sy[z]
        total_squares = jnp.sum(sy[z] * sy[z])
        for p in range(3):
            def body(i, sums):
                v = f32(out[p, pl.ds(pl.multiple_of(i * 16, 16), 16), :])
                return sums + jnp.sum(v * v)

            total_squares = lax.fori_loop(0, rows // 16, body, total_squares)
        norms[w] = jnp.full((8, 128), total_squares, jnp.float32)
        for k in range(1, 8):
            sends.start(None, lambda k=k: copy(norms.at[w], norms.at[w], n_s.at[k], n_r.at[w], (peer(k), x * 2 + c)))
        for k in range(1, 8):
            wait(None, norms.at[peer(k)], n_r.at[peer(k)])
        whole = norms[0]
        for k in range(1, 8):
            whole = whole + norms[k]
        norm_out[...] = jnp.sqrt(whole)

    def looped(n, body, steps):
        @pl.loop(0, n)
        def _(i):
            body(i)
            for k in sorted(steps):
                pl.when(i == k)(lambda k=k: [step() for step in steps[k]] and None)

    bar = pltpu.get_barrier_semaphore()
    for to in [near, over, diag] + [(peer(k), x * 2 + c) for k in range(1, 8)]:
        pl.semaphore_signal(bar, inc=1, device_id=to, device_id_type=MESH)
    pl.semaphore_wait(bar, 10)

    need(L_DLOW, L_ACT)
    transpose_into(dlow)
    for zz in ORDER:
        grads(0, zz, act_m)
    need(L_DOWN, L_SLOPE)
    for k in range(4):
        upper_back(k)
    need(L_HID)
    transpose_into(hid_m)
    for k in range(4):
        dup_copy(k).wait_recv()
    for zz in ORDER:
        grads(1, zz, dupper)
    need(L_UP, L_DTWO, L_NORMED, L_INV, L_ATTN, L_DVEC)
    hidden_back()
    need(L_QUERY, L_KV)
    P = functools.partial
    looped(seqs * 6, attend_back, {2: [P(add_x, 0, 3)], 5: [P(add_x, 0, 0)], 8: [P(add_x, 0, 2)], 11: [P(add_x, 0, 1)]})
    swap(dquery, 1)
    small_start()
    need(L_TOKENS, L_ROWS, L_MIXED)
    key_value_grads()
    for make in swaps:
        make().wait_recv()
    attention_sides()
    for zz in ORDER:
        attention_grads(zz)
    masked_tokens()
    tile = total // 256
    looped(tile, tokens_back, {0: [P(add_y, 0, 3), small_x], 1: [P(add_y, 0, 0)], 2: [P(add_y, 0, 2)], 3: [P(add_y, 0, 1), small_y]})
    for i in range(tile - 2, tile):
        token_store(i).wait()
    tile_load(0).start()
    looped(tile * 4, feed_forward, {
        0: [P(add_x, 1, 3), P(add_x, 1, 0)],
        1: [P(line, 0, 0), small_add],
        2: [P(add_x, 1, 2), P(add_x, 1, 1), P(line, 0, 1)],
        3: [P(line, 0, 2), small_line],
        4: [P(add_y, 1, 3), P(owner, 0)],
        5: [P(add_y, 1, 0)],
        6: [P(add_y, 1, 2), P(add_x, 2, 3)],
        7: [P(add_y, 1, 1), P(add_x, 2, 0)],
        8: [P(line, 1, 0), P(add_x, 2, 2)],
        9: [P(line, 1, 1), P(add_x, 2, 1)],
        10: [P(line, 1, 2), P(middle_x, 0)],
        11: [P(owner, 1)],
        12: [P(add_y, 2, 3)],
        13: [P(add_y, 2, 0)],
        14: [P(middle_x, 1)],
        15: [P(add_y, 2, 2)],
    })
    add_y(2, 1)
    for t in range(3):
        line(2, t)
    owner(2)
    middle_x(2)
    for i in range(tile - 2, tile):
        layer_store(i).wait()
    for p in range(3):
        arrived(p)
    square_sum()
    sends.finish()
    for make in swaps:
        make().wait_send()
    for k in range(4):
        dup_copy(k).wait_send()


def backward(attn, up, down, vec, bias, kv, hidden, query_m, rows_m, mixed_m, hid_m, act_m, slope, dtwo, dlow, normed, inverse, dvec, tokens, spots):
    total, width = hidden.shape
    cols = up.shape[1]
    rows = width // 8
    seqs, padded = spots.shape
    length = total // seqs
    count = seqs * padded
    shape = jax.ShapeDtypeStruct
    f = jnp.float32
    anywhere = pl.BlockSpec(memory_space=pl.ANY)
    vm = pl.BlockSpec(memory_space=pltpu.VMEM)
    dma = pltpu.SemaphoreType.DMA
    v = pltpu.VMEM
    inputs = (attn, up, down, vec, bias, kv, hidden, query_m, rows_m, mixed_m, hid_m, act_m, slope, dtwo, dlow, normed, inverse, dvec, tokens, spots)

    def like(a):
        return v(a.shape, a.dtype)

    one = (16, 128)
    scratch = [like(a) for a in (attn, up, down, kv, query_m, rows_m, mixed_m, hid_m, act_m, slope, dtwo, dlow, normed, inverse, dvec, tokens)]
    scratch += [
        v((2, width, count), LOW), v((2, count, width), LOW), v((2, count, cols), LOW), v((1, cols), f), v((count, width), f), v((count, width), f),
        v((2, count, width), LOW), v((count, width), LOW), v((2, count, width), LOW), v((2, total, width), LOW), v((width, M), LOW), v((width, total), LOW),
        v((2, 256, width), f), v((256, width), f), v((2, 256, width), LOW),
        v((3, width, M), LOW), v((3, width, E), LOW), v((3, 4, rows, M), LOW), v((3, 5, rows, M), LOW), v((3, rows, M), LOW),
        v((8,) + one, f), v((8,) + one, f), v((8,) + one, f), v((8,) + one, f), v((4,) + one, f), v((4,) + one, f), v((4,) + one, f), v((8, 8, 128), f),
        dma((16,)), dma((2,)), dma((4,)), dma((2,)), dma((2,)), dma((4,)), dma((4,)), dma((4,)), dma((4,)), dma((3, 4)), dma((3, 4)), dma((3, 4)), dma((3, 4)),
        dma((2, 3, 4)), dma((2, 3, 4)), dma((3,)), dma((3,)), dma((3, 3)), dma((3, 3)), dma((14,)), dma((14,)), dma((8,)), dma((8,)),
    ]
    specs = [anywhere] * len(inputs)
    specs[3] = specs[4] = specs[19] = vm
    return pl.pallas_call(
        functools.partial(backward_kernel, rows, seqs, length, padded),
        out_shape=(shape((total, width), LOW), shape((total, width), f), shape((3, rows, cols), LOW), shape(one, f), shape((8, 128), f)),
        in_specs=specs,
        out_specs=(anywhere, anywhere, vm, vm, vm),
        scratch_shapes=scratch,
        compiler_params=pltpu.CompilerParams(collective_id=1, has_side_effects=True, vmem_limit_bytes=64 * 2**20 - 2**16),
    )(*inputs)


def masks(mask_place, mask_count, gradient, length):
    seqs, slots = mask_place.shape
    padded = -(-slots // 16) * 16
    live = jnp.arange(padded)[None, :] < mask_count[:, None]
    spots = jnp.pad(mask_place, ((0, 0), (0, padded - slots)), constant_values=-1)
    pick = (spots[:, :, None] == jnp.arange(length)[None, None, :]) & live[:, :, None]
    gradient = jnp.pad(gradient, ((0, 0), (0, padded - slots), (0, 0)))
    gradient = jnp.where(live[:, :, None], gradient, jnp.zeros_like(gradient))
    return pick, jnp.where(live, spots, -1), gradient.reshape(seqs * padded, -1)


def update(weights, moments, grads, grad_norm):
    factor = CLIP_LIMIT / jnp.maximum(grad_norm, CLIP_LIMIT)
    rates = (LEARN_RATE, OUTPUT_RATE, LEARN_RATE, LEARN_RATE, VECTOR_RATE, BIAS_RATE)
    out = ()
    for k in range(6):
        out += adam_step(weights[k], *moments[k], grads[k], factor, DECAY_RATE if k < 4 else 0.0, rates[k])
    return out


def natural(own_attn, own_up, own_down, own_vectors, own_bias):
    width = own_up.shape[1] // 4
    own_qkv = jnp.swapaxes(own_attn[:, : 3 * width].reshape(-1, 3, width), 0, 1)
    return own_qkv, own_attn[:, 3 * width :].T, own_up, own_down.T, own_vectors, own_bias


def pack(qkv, out, up, down):
    attn = jnp.concatenate([qkv[0], qkv[1], qkv[2], out.T], axis=1)
    return attn.astype(jnp.bfloat16), up.astype(jnp.bfloat16), down.T.astype(jnp.bfloat16)


def small_pack(vectors, bias):
    rows = vectors.shape[1]
    return jnp.concatenate([jnp.pad(vectors, ((0, 0), (0, 128 - rows))), bias.reshape(-1, 128), jnp.zeros((5, 128))])


def plain(tokens, pick, spots, gradient, weights):
    low = jnp.bfloat16
    seqs, length, width = tokens.shape
    padded = pick.shape[1]
    flat = tokens.reshape(seqs * length, width)
    attn_w, up_w, down_w = (lax.all_gather(v, "wide", axis=0, tiled=True) for v in pack(*weights[:4]))
    vec = lax.all_gather(weights[4].astype(low), "wide", axis=1, tiled=True).astype(jnp.float32)
    bias = lax.all_gather(weights[5].astype(low), "wide", axis=0, tiled=True).astype(jnp.float32)
    wq, wk, wv, wo = (attn_w[:, k * width : (k + 1) * width] for k in range(4))
    query = (mm(flat, wq, NN) + vec[0]).astype(low)
    key = mm(flat, wk, NN, low)
    value = (mm(flat, wv, NN) + vec[1]).astype(low)
    query, key, value = (split_heads(v, seqs, length) for v in (query, key, value))
    mixed = lax.map(attend, (query, key, value)).reshape(seqs * length, width)

    def middle(rows, mixed):
        pre_one = rows.astype(jnp.float32) + (mm(mixed, wo, NT) + vec[2])
        hidden, normed, inverse = layer_norm(pre_one, vec[3], vec[4])
        hidden_low = hidden.astype(low)
        upper = mm(hidden_low, up_w, NN) + bias
        cumul = 0.5 * (1.0 + lax.erf(upper * SQRT_HALF))
        active = (upper * cumul).astype(low)
        pre_two = hidden + (mm(active, down_w, NT) + vec[5])
        return layer_norm(pre_two, vec[6], vec[7]), normed, inverse, hidden_low, upper, cumul, active

    layer_out = middle(flat, mixed)[0][0].astype(low)
    pick_low = pick.astype(low)

    def take(values):
        values = values.reshape(seqs, length, width)
        return jnp.einsum("sil,sld->sid", pick_low, values, preferred_element_type=jnp.float32).astype(low)

    rows_m = take(flat).reshape(seqs * padded, width)
    mixed_m = take(mixed).reshape(seqs * padded, width)
    query_m = split_heads(take(query), seqs, padded)
    (_, normed_two, inverse_two), normed_one, inverse_one, hidden_m, upper, cumul, active = middle(rows_m, mixed_m)
    dpre_two, dgain_two, dshift_two = norm_back(gradient.astype(jnp.float32), normed_two, inverse_two, vec[6])
    dbias_two = jnp.sum(dpre_two, axis=0)
    dtwo_low = dpre_two.astype(low)
    ddown = mm(dtwo_low, active, TN)
    dactive = mm(dtwo_low, down_w, NN)
    density = jnp.exp(-0.5 * upper * upper) * INV_ROOT_TWO_PI
    dupper = dactive * (cumul + upper * density)
    dup_bias = jnp.sum(dupper, axis=0)
    dupper_low = dupper.astype(low)
    dup = mm(hidden_m, dupper_low, TN)
    dhidden = dpre_two + mm(dupper_low, up_w, NT)
    dpre_one, dgain_one, dshift_one = norm_back(dhidden, normed_one, inverse_one, vec[3])
    dbias_out = jnp.sum(dpre_one, axis=0)
    done_low = dpre_one.astype(low)
    dout = mm(done_low, mixed_m, TN)
    dmixed = split_heads(mm(done_low, wo, NN, low), seqs, padded)
    dquery, dkey, dvalue = lax.map(attend_back, (query_m, key, value, dmixed))
    dquery = dquery.reshape(seqs * padded, width)
    dkey = dkey.reshape(seqs * length, width)
    dvalue = dvalue.reshape(seqs * length, width)
    dbias_query = jnp.sum(dquery, axis=0)
    dbias_value = jnp.sum(dvalue, axis=0)
    dquery, dkey, dvalue = dquery.astype(low), dkey.astype(low), dvalue.astype(low)
    dattn = jnp.concatenate([mm(rows_m, dquery, TN), mm(flat, dkey, TN), mm(flat, dvalue, TN), dout], axis=1)
    masked_part = dpre_one + mm(dquery, wq, NT)
    dtokens = spread(pick, masked_part) + mm(dkey, wk, NT) + mm(dvalue, wv, NT)
    dvectors = jnp.stack(
        [dbias_query, dbias_value, dbias_out, dgain_one, dshift_one, dbias_two, dgain_two, dshift_two]
    )

    def owned(value, dim):
        return lax.psum(lax.psum_scatter(value, "wide", scatter_dimension=dim, tiled=True), "narrow")

    grads = (owned(dattn, 0), owned(dup, 0), owned(ddown, 0), owned(dvectors, 1), owned(dup_bias, 0))
    grad_norm = jnp.sqrt(lax.psum(sum(jnp.sum(v * v) for v in grads), "wide"))
    return layer_out, dtokens, grads, grad_norm


def spread(pick, rows):
    seqs, padded, length = pick.shape
    return jnp.einsum(
        "sil,sid->sld",
        pick.astype(jnp.float32),
        rows.reshape(seqs, padded, -1),
        precision=lax.Precision.HIGHEST,
        preferred_element_type=jnp.float32,
    ).reshape(seqs * length, -1)


def tailored(tokens, pick, spots, gradient, weights):
    low = jnp.bfloat16
    seqs, length, width = tokens.shape
    flat = tokens.reshape(seqs * length, width)
    saved = forward(*pack(*weights[:4]), small_pack(*weights[4:]).astype(low), flat, pick.astype(low), gradient)
    layer_out, dtokens, own, small, grad_norm = backward(*saved, flat, spots)
    own = own.astype(jnp.float32)
    rows = own.shape[1]
    return layer_out, dtokens, (own[2], own[1], own[0], small[:8, :rows], small[8:11].reshape(-1)), grad_norm[0, 0]


def shards(body, tokens, mask_place, mask_count, masked_output_gradient, *parameters):
    seqs, length, width = tokens.shape
    weights = parameters[0::3]
    moments = tuple(zip(parameters[1::3], parameters[2::3]))
    pick, spots, gradient = masks(mask_place, mask_count, masked_output_gradient, length)
    layer_out, dtokens, grads, grad_norm = body(tokens, pick, spots, gradient, weights)
    layer_out, dtokens = (v.reshape(seqs, length, width) for v in (layer_out, dtokens))
    return (layer_out, dtokens, grad_norm) + update(weights, moments, natural(*grads), grad_norm)


def solution(mesh):
    body = tailored if mesh.shape["wide"] == 8 and mesh.shape["narrow"] == 4 else plain
    data = P(("wide", "narrow"))
    rows = P("wide")
    columns = P(None, "wide")
    weights = (columns,) * 6 + (rows,) * 3 + (columns,) * 6 + (rows,) * 3
    return jax.shard_map(
        functools.partial(shards, body),
        mesh=mesh,
        in_specs=(data,) * 4 + weights,
        out_specs=(data, data, P()) + weights,
        check_vma=False,
    )
```

profile of v0, /device:TPU:0, one launch (start us, length us, event | category | flops | bytes accessed | tf_op | source)
XLA Modules:
  0.0 263.8 jit_solution(5871315659867173662)
XLA Ops:
  0.7 0.8 iota_compare_fusion.2
  3.6 1.3 broadcast_select_fusion.1
  5.0 1.0 convert_bitcast_fusion.1
  6.0 0.8 fusion.8.pick
  6.8 1.3 broadcast_select_fusion
  8.1 0.7 copy.56
  8.9 0.9 pad_maximum_fusion.attn
  10.4 0.9 convert_element_type.20.up
  11.3 0.9 convert_bitcast_fusion.down
  12.1 81.7 %shard_map.373 = (bf16[768,3072]{1,0:T(8,128)(2,1)}, bf16[768,3072]{1,0:T(8,128)(2,1)}, bf16[768,3072]{1,0:T(8,128)(2,1)}, f32[8,768]{1,0:T(8,128)}, f32[1,3072]...) custom-call(bf16[96,3072]{1,0:T(8,128)(2,1)} %pad_maximum_fusion.att, ...), custom_call_target="tpu_custom_call" | custom-call | tf_op jit(solution)/shard_map/pallas_call | solution.py:662
  93.8 147.5 %shard_map.374 = (bf16[1024,768]{1,0:T(8,128)(2,1)}, f32[1024,768]{1,0:T(8,128)}, bf16[3,96,3072]{2,1,0:T(8,128)(2,1)}, f32[16,128]{1,0:T(8,128)}, f32[8,128]{1,0:T(8,128)}) custom-call(bf16[768,3072]{1,0:T(8,128)(2,1)} %get-tuple-element.44.attn_h, bf16[768,3072]{1,0:T(8,128)(2,1)} %get-tuple-element.45.up_h, bf16[768,3072]{1,0:T(8,128)(2,1)} %get-tuple-element.46.down_h, ...), custom_call_target="tpu_custom_call" | custom-call | tf_op jit(solution)/shard_map/pallas_call | solution.py:1229
  241.4 1.2 slice.39
  243.3 1.3 multiply_subtract_fusion.5
  244.6 1.3 multiply_subtract_fusion.4
  245.9 1.9 convert_element_type.24
  248.0 0.8 copy-done.8
  249.1 1.1 multiply_subtract_fusion.3
  250.9 1.9 multiply_subtract_fusion.2
  253.8 2.4 multiply_subtract_fusion
  256.2 0.8 copy-done.12
  257.1 2.4 multiply_subtract_fusion.1
  259.5 1.1 copy.65
  260.6 1.3 copy-done.6
  261.9 1.7 copy.66
  (41 shorter events, 5.0 us)
Async XLA Ops:
  0.7 8.2 %copy-start.4 = (f32[3,96,768]{2,1,0:T(8,128)S(1)}, f32[3,96,768]{2,1,0:T(8,128)}, u32[]{:S(2)}) copy-start(f32[3,96,768]{2,1,0:T(8,128)} %param.26) | copy-start | bytes 2654212
  8.9 1.5 copy-start.2
  8.9 2.3 copy-start
  247.9 1.0 copy-start.8
  247.9 1.0 copy-start.15
  247.9 1.1 copy-start.16
  247.9 2.2 copy-start.14
  249.1 1.6 copy-start.5
  249.1 1.8 copy-start.13
  250.9 1.9 copy-start.1
  250.9 2.6 copy-start.9
  250.9 2.9 %copy-start.10 = (f32[3072,96]{0,1:T(8,128)S(1)}, f32[3072,96]{0,1:T(8,128)}, u32[]{:S(2)}) copy-start(f32[3072,96]{0,1:T(8,128)} %param.37) | copy-start | bytes 3538948
  253.8 2.4 copy-start.3
  253.8 2.4 copy-start.11
  253.8 3.3 %copy-start.12 = (f32[96,3072]{1,0:T(8,128)S(1)}, f32[96,3072]{1,0:T(8,128)}, u32[]{:S(2)}) copy-start(f32[96,3072]{1,0:T(8,128)} %param.34) | copy-start | bytes 3538948
  257.1 2.4 copy-start.7
  259.5 2.5 copy-start.6
where the time goes:
time: 268 us; the launch traced here: 264 us
  Pallas kernels  229 us (85%)
  other arithmetic  22.3 us (8%)
  local copies, waits for them, and re-layouts  10.6 us (4%)
    pallas_call x1, Pallas kernels, backward(): pl.pallas_call(functools.partial(backward_kernel, rows, seqs, length, pad...  148 us
    pallas_call x1, Pallas kernels, forward(): pl.pallas_call(functools.partial(forward_kernel, rows, seqs, length, padd...  81.7 us
    sub x6, other arithmetic, adam_step(): weight - rate * (mean_hat / (jnp.sqrt(square_hat) + ADAM_EPS) + decay * w...  10.5 us
    unnamed x36, local copies, waits for them, and re-layouts  8.35 us

commit v1 on v0

--- a/solution.py
+++ b/solution.py
@@ -344,20 +344,21 @@
 
 def forward_kernel(
     rows, seqs, length, padded,
-    attn, up, down, small, tokens, pick, grad,
-    attn_o, up_o, down_o, vec_o, bias_o, kv_o, hidden_o, query_o, rows_o, mixed_o, hid_o, act_o, slope_o, dtwo_o, dlow_o, normed_o, inv_o, dvec_o,
-    attn_full, up_full, down_full, small_full,
+    qkv_h, out_h, up_h, down_h, vectors, up_bias, tokens_h, place_m, count_m, grad_m,
+    attn_o, up_o, down_o, vec_o, bias_o, kv_o, hidden_o, query_o, rows_o, mixed_o, hid_o, act_o, slope_o, dtwo_o, dlow_o, normed_o, inv_o, dvec_o, pick_o,
+    attn_full, up_full, down_full, small_full, small_f, qkv_f, out_f, up_f, down_f, tokens, pick, pick_t, grad,
     qkv, mixed, hidden, vec, qbias, bias, query_m, rows_m, mixed_m, hid_m, act_m, slope, ytwo, dtwo, dlow, dvec, hid_f, normed_one, inverse_one,
-    send_sem, recv_sem, small_send, small_recv, own_sem, save_sem, pair_send, pair_recv,
+    send_sem, recv_sem, small_send, small_recv, load_sem, save_sem, pair_send, pair_recv,
 ):
     z, y, x, c = place()
     width = tokens.shape[1]
-    cols = attn.shape[1]
+    cols = up_h.shape[1]
     edge = x == c
     third = cols // 3
     mine, across = x + c, 2 * flip(x)
     fulls = (attn_full, up_full, down_full)
-    shards = (attn, up, down)
+    w = z * 2 + y
+    mine_rows = pl.ds(pl.multiple_of(w * rows, 32), rows)
     sends = Sends()
     zl, zh = z > 0, z < 3
     count = seqs * padded
@@ -365,48 +366,26 @@
     def spot(p, zz, yy, t):
         return fulls[p].at[pl.ds(pl.multiple_of((zz * 2 + yy) * rows, rows), rows), pl.ds(pl.multiple_of(t * third, third), third)]
 
-    def push(cond, p, zz, yy, t, kind, to, src=None):
+    def push(cond, p, zz, yy, t, kind, to):
         def make():
-            w = zz * 2 + yy
+            whose = zz * 2 + yy
             where = spot(p, zz, yy, t)
             return pltpu.make_async_remote_copy(
-                src_ref=where if src is None else src,
+                src_ref=where,
                 dst_ref=where,
-                send_sem=send_sem.at[kind, p, w],
-                recv_sem=recv_sem.at[p, w, t],
+                send_sem=send_sem.at[kind, p, whose],
+                recv_sem=recv_sem.at[p, whose, t],
                 device_id=to,
                 device_id_type=MESH,
             )
 
         sends.start(cond, make)
 
-    def small_push(cond, zz, yy, kind, to, src=None):
-        def make():
-            w = zz * 2 + yy
-            where = small_full.at[w]
-            return pltpu.make_async_remote_copy(
-                src_ref=where if src is None else src,
-                dst_ref=where,
-                send_sem=small_send.at[kind, w],
-                recv_sem=small_recv.at[w],
-                device_id=to,
-                device_id_type=MESH,
-            )
-
-        sends.start(cond, make)
-
     def arrive(cond, p, zz, yy, t):
         def body():
             where = spot(p, zz, yy, t)
-            w = zz * 2 + yy
-            pltpu.make_async_remote_copy(where, where, send_sem.at[0, p, w], recv_sem.at[p, w, t], dev(z, y, x, c), device_id_type=MESH).wait_recv()
-
-        when(cond, body)
-
-    def small_arrive(cond, zz, yy):
-        def body():
-            w = zz * 2 + yy
-            pltpu.make_async_remote_copy(small_full.at[w], small_full.at[w], small_send.at[0, w], small_recv.at[w], dev(z, y, x, c), device_id_type=MESH).wait_recv()
+            whose = zz * 2 + yy
+            pltpu.make_async_remote_copy(where, where, send_sem.at[0, p, whose], recv_sem.at[p, whose, t], dev(z, y, x, c), device_id_type=MESH).wait_recv()
 
         when(cond, body)
 
@@ -418,10 +397,9 @@
         return ((None, z),) if d == 0 else ((z - d >= 0, z - d), (z + d <= 3, z + d))
 
     def own(p):
-        src = shards[p].at[:, pl.ds(pl.multiple_of(mine * third, third), third)]
-        push(zh, p, z, y, mine, UP, above, src)
-        push(zl, p, z, y, mine, DOWN, below, src)
-        push(None, p, z, y, mine, SIDE, beside, src)
+        push(zh, p, z, y, mine, UP, above)
+        push(zl, p, z, y, mine, DOWN, below)
+        push(None, p, z, y, mine, SIDE, beside)
 
     def z_step(p, d):
         for cond, zz, onward, kind, to in ((z - d >= 0, z - d, zh, UP, above), (z + d <= 3, z + d, zl, DOWN, below)):
@@ -451,14 +429,7 @@
                 for cond, zz in () if d == 0 and yy is y else around(d):
                     arrive(cond, p, zz, yy, x + flip(c))
                     arrive(both(cond, edge), p, zz, yy, across)
-        copies[p].wait()
         keep(fulls[p], (attn_o, up_o, down_o)[p], p)
-
-    def small_z(d):
-        for cond, zz, onward, kind, to in ((z - d >= 0, z - d, zh, UP, above), (z + d <= 3, z + d, zl, DOWN, below)):
-            small_arrive(cond, zz, y)
-            small_push(both(cond, onward), zz, y, kind, to)
-            small_push(cond, zz, y, SIDE, beside)
 
     saves = []
 
@@ -476,19 +447,64 @@
         make().start()
         swaps.append((make, ref))
 
-    def vectors():
-        for d in range(4):
-            for cond, zz in around(d):
-                small_arrive(cond, zz, flip(y))
-        copies[3].wait()
+    def peer(k):
+        return lax.rem(w + k, 8)
+
+    def small_copy(k, whose):
+        return pltpu.make_async_remote_copy(
+            small_full.at[whose], small_full.at[whose], small_send.at[k], small_recv.at[whose], (peer(k), x * 2 + c), device_id_type=MESH
+        )
+
+    def small_out():
+        small_f[...] = jnp.zeros_like(small_f)
+        small_f[0:8, 0:rows] = vectors[...]
+        for r in range(3):
+            small_f[8 + r : 9 + r, :] = up_bias[pl.ds(r * 128, 128)].reshape(1, 128)
+        small_full[w] = small_f[...].astype(LOW)
+        for k in range(1, 8):
+            sends.start(None, lambda k=k: small_copy(k, w))
+
+    def attn_shard():
+        loads[0].wait()
+        loads[1].wait()
+        for k in range(3):
+            attn_full[mine_rows, pl.ds(k * width, width)] = qkv_f[k].astype(LOW)
+        attn_full[mine_rows, pl.ds(3 * width, width)] = out_f[...].astype(LOW)
+
+    def up_shard():
+        loads[2].wait()
+        up_full[mine_rows, :] = up_f[...].astype(LOW)
+
+    def down_shard():
+        loads[3].wait()
+        down_full[mine_rows, :] = down_f[...].astype(LOW)
+
+    def masks():
+        slots = place_m.shape[1]
+        for s in range(seqs):
+            hit = lax.broadcasted_iota(jnp.int32, (length, slots), 0) == place_m[s : s + 1, :]
+            live = lax.broadcasted_iota(jnp.int32, (length, slots), 1) < count_m[s]
+            hit = jnp.logical_and(hit, live).astype(jnp.float32).astype(LOW)
+            row = lax.broadcasted_iota(jnp.int32, (padded, slots), 0)
+            slot = lax.broadcasted_iota(jnp.int32, (padded, slots), 1)
+            same = (row == slot).astype(jnp.float32).astype(LOW)
+            kept = jnp.logical_and(row == slot, slot < count_m[s]).astype(jnp.float32).astype(LOW)
+            pick[s] = dot(same, hit, NT).astype(LOW)
+            pick_t[s] = dot(hit, same, NT).astype(LOW)
+            grad[pl.ds(s * padded, padded), :] = dot(kept, grad_m[s], NN)
+        keep(pick_t, pick_o, 18)
+
+    def vectors_in():
+        for k in range(1, 8):
+            small_copy(k, peer(k)).wait_recv()
         at = lax.broadcasted_iota(jnp.int32, (128, width), 0)
         to = lax.broadcasted_iota(jnp.int32, (128, width), 1)
         total = jnp.zeros((16, width), jnp.float32)
-        for w in range(8):
-            place_w = jnp.logical_and(at + w * rows == to, at < rows).astype(jnp.float32).astype(LOW)
-            total += dot(small_full[w], place_w, NN)
+        for k in range(8):
+            place_k = jnp.logical_and(at + k * rows == to, at < rows).astype(jnp.float32).astype(LOW)
+            total += dot(small_full[k], place_k, NN)
             for r in range(3):
-                bias[:, pl.ds(w * 384 + r * 128, 128)] = small_full[w, 8 + r : 9 + r, :].astype(jnp.float32)
+                bias[:, pl.ds(k * 384 + r * 128, 128)] = small_full[k, 8 + r : 9 + r, :].astype(jnp.float32)
         vec[...] = total[:8]
         qbias[0] = total[0:1]
         qbias[1] = jnp.zeros((1, width), jnp.float32)
@@ -567,7 +583,7 @@
 
         pre = hid_f[...] + (ytwo[...] + vec[5:6, :])
         _, normed, inverse = norm(pre, vec[6:7, :], vec[7:8, :])
-        value, dgain, dshift = norm_pull(grad[...].astype(jnp.float32), normed, inverse, vec[6:7, :])
+        value, dgain, dshift = norm_pull(grad[...], normed, inverse, vec[6:7, :])
         dtwo[...] = value
         dlow[0] = value.astype(LOW)
         dvec[...] = jnp.zeros_like(dvec)
@@ -578,52 +594,53 @@
         keep(dtwo, dtwo_o, 7)
         keep(dvec, dvec_o, 8)
 
-    meet(z, y, x, c, False)
-    small_push(zh, z, y, UP, above, small)
-    small_push(zl, z, y, DOWN, below, small)
-    small_push(None, z, y, SIDE, beside, small)
+    loads = []
+    for k, (src, dst) in enumerate(((qkv_h, qkv_f), (out_h, out_f), (up_h, up_f), (down_h, down_f), (tokens_h, tokens))):
+        loads.append(pltpu.make_async_copy(src, dst, load_sem.at[k]))
+        loads[-1].start()
+    bar = pltpu.get_barrier_semaphore()
+    for to in [near, over] + [(peer(k), x * 2 + c) for k in range(1, 8)]:
+        pl.semaphore_signal(bar, inc=1, device_id=to, device_id_type=MESH)
+    attn_shard()
+    pl.semaphore_wait(bar, 9)
     own(0)
-    w = z * 2 + y
-    copies = []
-    for p in range(3):
-        copies.append(pltpu.make_async_copy(shards[p], fulls[p].at[pl.ds(pl.multiple_of(w * rows, rows), rows)], own_sem.at[p]))
-    copies.append(pltpu.make_async_copy(small, small_full.at[w], own_sem.at[3]))
-    for copy in copies:
-        copy.start()
-    for d in range(1, 4):
-        small_z(d)
+    small_out()
+    up_shard()
+    down_shard()
+    masks()
 
     def save_hidden():
         keep(hidden, hidden_o, 9)
         keep(qkv.at[pl.ds(1, 2)], kv_o, 10)
 
-    head = [
-        lambda: z_step(0, 1), lambda: own(1), lambda: y_step(0, 0), lambda: z_step(0, 2), lambda: y_step(0, 1), lambda: x_step(0, 0), lambda: z_step(0, 3),
-        lambda: y_step(0, 2), lambda: x_step(0, 1), vectors, lambda: z_step(1, 1), lambda: own(2), lambda: y_step(0, 3), lambda: x_step(0, 2), lambda: z_step(1, 2), lambda: y_step(1, 0), lambda: x_step(0, 3), lambda: z_step(1, 3),
-        lambda: last(0),
-    ]
-    links = [
-        lambda: y_step(1, 1), lambda: x_step(1, 0), lambda: z_step(2, 1), lambda: y_step(1, 2), lambda: x_step(1, 1), lambda: z_step(2, 2), lambda: y_step(1, 3), lambda: x_step(1, 2), lambda: z_step(2, 3),
-        lambda: y_step(2, 0), lambda: x_step(1, 3), lambda: y_step(2, 1), lambda: x_step(2, 0), lambda: y_step(2, 2),
-    ]
+    Z, Y, X, L = z_step, y_step, x_step, last
+    head = (
+        (Z, 0, 1), (Y, 0, 0), (Z, 0, 2), (Y, 0, 1), (X, 0, 0), (Z, 0, 3), (own, 1), (Y, 0, 2), (X, 0, 1), (vectors_in,), (Y, 0, 3), (X, 0, 2), (Z, 1, 1), (X, 0, 3), (L, 0),
+    )
+    links = (
+        (Y, 1, 0), (Z, 1, 2), (Y, 1, 1), (X, 1, 0), (Z, 1, 3), (own, 2), (Y, 1, 2), (X, 1, 1), (Y, 1, 3), (X, 1, 2), (Z, 2, 1), (X, 1, 3), (L, 1), (Y, 2, 0), (Z, 2, 2), (Y, 2, 1), (X, 2, 0), (Z, 2, 3),
+    )
+    ends = ((Y, 2, 2), (X, 2, 1), (Y, 2, 3), (X, 2, 2), (X, 2, 3))
     work = [functools.partial(project, i) for i in range(4)]
     work += [functools.partial(attend, s, j) for s in range(seqs) for j in range(width // 128)]
     work += [functools.partial(middle, i) for i in range(4)]
-    work += [masked_rows]
-    for step in head:
-        step()
+    work += [masked_rows, save_hidden]
+    for step, *rest in head:
+        step(*rest)
+    loads[4].wait()
     done = 0
-    for k, step in enumerate(links):
+    for k, (step, *rest) in enumerate(links):
         upto = len(work) * (k + 1) // len(links)
         for piece in work[done:upto]:
             piece()
         done = upto
-        step()
-    save_hidden()
-    last(1)
+        step(*rest)
     for k in range(4):
         upper(k)
-        (lambda: x_step(2, 1), lambda: y_step(2, 3), lambda: x_step(2, 2), lambda: x_step(2, 3))[k]()
+        step, *rest = ends[k]
+        step(*rest)
+    step, *rest = ends[4]
+    step(*rest)
     after_upper()
     last(2)
     lower()
@@ -640,11 +657,13 @@
         copy.wait()
 
 
-def forward(attn, up, down, small, tokens, pick, grad):
-    rows, cols = attn.shape
-    width = tokens.shape[1]
-    seqs, padded, length = pick.shape
-    total = tokens.shape[0]
+def forward(qkv, out, up, down, vectors, up_bias, tokens, place_m, count_m, grad_m):
+    rows, cols = up.shape
+    out, down = out.T, down.T
+    total, width = tokens.shape
+    seqs, slots = place_m.shape
+    length = total // seqs
+    padded = -(-slots // 16) * 16
     count = seqs * padded
     shape = jax.ShapeDtypeStruct
     f = jnp.float32
@@ -656,30 +675,36 @@
         full, full, full, shape((8, width), f), shape((1, cols), f), shape((2, total, width), LOW), shape((total, width), f),
         shape((count, width), LOW), shape((2, count, width), LOW), shape((2, count, width), LOW), shape((2, count, width), LOW),
         shape((2, count, cols), LOW), shape((count, cols), f), shape((count, width), f), shape((2, count, width), LOW),
-        shape((count, width), f), shape((count, 128), f), shape((8, width), f),
+        shape((count, width), f), shape((count, 128), f), shape((8, width), f), shape((seqs, length, padded), LOW),
     )
     v = pltpu.VMEM
     return pl.pallas_call(
         functools.partial(forward_kernel, rows, seqs, length, padded),
         out_shape=outs,
-        in_specs=[anywhere] * 4 + [vm] * 3,
+        in_specs=[anywhere] * 4 + [vm] * 2 + [anywhere, vm, pl.BlockSpec(memory_space=pltpu.SMEM), vm],
         out_specs=(anywhere,) * len(outs),
         scratch_shapes=[
-            v((8 * rows, cols), LOW), v((8 * rows, cols), LOW), v((8 * rows, cols), LOW), v((8, 16, 128), LOW),
+            v((8 * rows, cols), LOW), v((8 * rows, cols), LOW), v((8 * rows, cols), LOW), v((8, 16, 128), LOW), v((16, 128), f),
+            v(qkv.shape, f), v(out.shape, f), v(up.shape, f), v(down.shape, f), v(tokens.shape, LOW), v((seqs, padded, length), LOW), v((seqs, length, padded), LOW), v((count, width), f),
             v((3, total, width), LOW), v((total, width), LOW), v((total, width), f), v((8, width), f), v((3, 1, width), f), v((1, cols), f),
             v((count, width), LOW), v((2, count, width), LOW), v((2, count, width), LOW), v((2, count, width), LOW), v((2, count, cols), LOW),
             v((count, cols), f), v((count, width), f), v((count, width), f), v((2, count, width), LOW), v((8, width), f),
             v((count, width), f), v((count, width), f), v((count, 128), f),
-            dma((6, 3, 8)), dma((3, 8, 3)), dma((3, 8)), dma((8,)), dma((4,)), dma((18,)), dma((5,)), dma((5,)),
+            dma((6, 3, 8)), dma((3, 8, 3)), dma((8,)), dma((8,)), dma((5,)), dma((19,)), dma((5,)), dma((5,)),
         ],
         compiler_params=pltpu.CompilerParams(collective_id=0, has_side_effects=True, vmem_limit_bytes=60 * 2**20),
-    )(attn, up, down, small, tokens, pick, grad)
+    )(qkv, out, up, down, vectors, up_bias, tokens, place_m, count_m, grad_m)
 
 
 E = 768
 M = 1536
 SLAB = 32
 ORDER = (3, 0, 2, 1)
+BESIDE_ATTENTION = {1: (("add_x", 0, 3), ("grads", 1, 3),), 3: (("grads", 1, 0),), 4: (("add_x", 0, 0),), 5: (("grads", 1, 2),), 7: (("add_x", 0, 2), ("grads", 1, 1),), 10: (("add_x", 0, 1),)}
+BESIDE_KEYS = (("add_x", 1, 3), ("add_y", 0, 3), ("add_x", 1, 0),)
+BESIDE_TOKENS = {0: (("add_x", 1, 2), ("add_y", 0, 0), ("line", 0, 0),), 1: (("attention_grads", 3),), 2: (("add_x", 1, 1),), 3: (("add_y", 0, 2), ("attention_grads", 0),)}
+BESIDE_FEED_FORWARD = {0: (("add_x", 2, 3),), 1: (("attention_grads", 2),), 2: (("add_x", 2, 0), ("add_y", 0, 1), ("line", 0, 1),), 3: (("add_y", 1, 3), ("attention_grads", 1),), 4: (("add_x", 2, 2), ("add_y", 1, 0), ("line", 1, 0), ("add_y", 1, 2),), 6: (("line", 0, 2), ("add_x", 2, 1),), 8: (("add_y", 1, 1),), 9: (("line", 1, 1),), 12: (("add_y", 2, 3),), 13: (("owner", 0),)}
+LAST = (("add_y", 2, 0), ("line", 2, 0), ("line", 1, 2), ("add_y", 2, 2), ("add_y", 2, 1), ("owner", 1), ("line", 2, 1), ("line", 2, 2), ("middle_x", 0), ("owner", 2), ("arrived", 0), ("middle_x", 1), ("arrived", 1), ("middle_x", 2), ("arrived", 2),)
 
 
 def slabs(rows, body):
@@ -694,14 +719,14 @@
 
 def backward_kernel(
     rows, seqs, length, padded,
-    attn_h, up_h, down_h, vec, bias, kv_h, hidden_h, query_h, rows_h, mixed_h, hid_h, act_h, slope_h, dtwo_h, dlow_h, normed_h, inv_h, dvec_h, tokens_h, spots,
+    attn_h, up_h, down_h, vec, bias, kv_h, hidden_h, query_h, rows_h, mixed_h, hid_h, act_h, slope_h, dtwo_h, dlow_h, normed_h, inv_h, dvec_h, pick_h, tokens_h,
     layer_h, dtokens_h, out, small_out, norm_out,
-    attn, up, down, kv, query_m, rows_m, mixed_m, hid_m, act_m, slope, dtwo, dlow, normed, inverse, dvec, tokens,
+    attn, up, down, kv, query_m, rows_m, mixed_m, hid_m, act_m, slope, dtwo, dlow, normed, inverse, dvec, pick_t, tokens,
     left, right, dupper, dbias, dhid, dpre, done, dmix, dquery, dkv, part, tokens_t,
     htile, ytile, ltile,
     acc, xb, yr, zr, mr,
-    sall, sall2, ssib, sx, sy, szu, szd, norms,
-    load_sem, tile_sem, out_sem, pair_s, pair_r, dup_s, dup_r, sib_s, sib_r, x_s, x_r, y_s, y_r, z_s, z_r, m_s, m_r, f_s, f_r, sm_s, sm_r, n_s, n_r,
+    sall, sall2, ssib, sx, sy, norms,
+    load_sem, tile_sem, out_sem, pair_s, pair_r, dup_s, dup_r, sib_s, sib_r, x_s, x_r, y_s, y_r, z_s, z_r, m_s, m_r, f_s, f_r, sm_s, sm_r, sy_r, n_s, n_r,
 ):
     z, y, x, c = place()
     edge = x == c
@@ -720,11 +745,11 @@
     loads = []
     for k, (src, dst) in enumerate((
         (dlow_h, dlow), (act_h, act_m), (down_h, down), (slope_h, slope), (hid_h, hid_m), (up_h, up), (dtwo_h, dtwo), (normed_h, normed),
-        (inv_h, inverse), (dvec_h, dvec), (attn_h, attn), (mixed_h, mixed_m), (query_h, query_m), (kv_h, kv), (rows_h, rows_m), (tokens_h, tokens),
+        (inv_h, inverse), (dvec_h, dvec), (attn_h, attn), (mixed_h, mixed_m), (query_h, query_m), (kv_h, kv), (rows_h, rows_m), (tokens_h, tokens), (pick_h, pick_t),
     )):
         loads.append(pltpu.make_async_copy(src, dst, load_sem.at[k]))
         loads[-1].start()
-    (L_DLOW, L_ACT, L_DOWN, L_SLOPE, L_HID, L_UP, L_DTWO, L_NORMED, L_INV, L_DVEC, L_ATTN, L_MIXED, L_QUERY, L_KV, L_ROWS, L_TOKENS) = range(16)
+    (L_DLOW, L_ACT, L_DOWN, L_SLOPE, L_HID, L_UP, L_DTWO, L_NORMED, L_INV, L_DVEC, L_ATTN, L_MIXED, L_QUERY, L_KV, L_ROWS, L_TOKENS, L_PICK) = range(17)
 
     def need(*ks):
         for k in ks:
@@ -1039,8 +1064,7 @@
 
         r = pl.ds(pl.multiple_of(i * 256, 256), 256)
         s = i // (length // 256)
-        here = lax.broadcasted_iota(jnp.int32, (256, padded), 0) + lax.rem(i, length // 256) * 256
-        pick = (here == spots[pl.ds(s, 1), :]).astype(jnp.float32).astype(LOW)
+        pick = pick_t[s, pl.ds(pl.multiple_of(lax.rem(i, length // 256) * 256, 256), 256), :]
         value = dpre[pl.ds(pl.multiple_of(s * padded, padded), padded), :]
         high = value.astype(LOW)
         rest = (value - f32(high)).astype(LOW)
@@ -1064,48 +1088,39 @@
         ssib[...] = sall[...] + ssib[...]
         sends.start(None, lambda: copy(ssib, sx, sm_s.at[1], sm_r.at[1], over))
 
+    w = z * 2 + y
+
+    def peer(k):
+        return lax.rem(w + k, 8)
+
     def small_y():
         wait(None, sx, sm_r.at[1])
         sall2[...] = ssib[...] + sx[...]
-        for zz in range(4):
-            sends.start(None, lambda zz=zz: copy(sall2.at[zz * 2 + flip(y)], sy.at[zz], sm_s.at[2 + zz], sm_r.at[2 + zz], beside))
+        for k in range(1, 8):
+            sends.start(None, lambda k=k: copy(sall2.at[peer(k)], sy.at[w], sm_s.at[1 + k], sy_r.at[w], (peer(k), x * 2 + c)))
+        sy[w] = sall2[w]
 
     def small_add():
-        for zz in range(4):
-            wait(None, sy.at[zz], sm_r.at[2 + zz])
-            sy[zz] = sy[zz] + sall2[zz * 2 + y]
-
-    def small_line():
-        for zz in ORDER:
-            @pl.when(both(z <= zz, z > 0))
-            def _():
-                wait(None, szu.at[zz], sm_r.at[6 + zz])
-                sy[zz] = sy[zz] + szu[zz]
-
-            sends.start(lambda zz=zz: z < zz, lambda zz=zz: copy(sy.at[zz], szu.at[zz], sm_s.at[6 + zz], sm_r.at[6 + zz], above))
-
-            @pl.when(both(z >= zz, z < 3))
-            def _():
-                wait(None, szd.at[zz], sm_r.at[10 + zz])
-                sy[zz] = sy[zz] + szd[zz]
-
-            sends.start(lambda zz=zz: z > zz, lambda zz=zz: copy(sy.at[zz], szd.at[zz], sm_s.at[10 + zz], sm_r.at[10 + zz], below))
-
-    w = z * 2 + y
-
-    def peer(k):
-        return lax.rem(w + k, 8)
+        for k in range(1, 8):
+            wait(None, sy.at[peer(k)], sy_r.at[peer(k)])
+        value = sy[0]
+        for k in range(1, 8):
+            value = value + sy[k]
+        small_out[...] = value
 
     def square_sum():
-        small_out[...] = sy[z]
-        total_squares = jnp.sum(sy[z] * sy[z])
+        value = small_out[...]
+        squares = value * value
         for p in range(3):
             def body(i, sums):
                 v = f32(out[p, pl.ds(pl.multiple_of(i * 16, 16), 16), :])
-                return sums + jnp.sum(v * v)
-
-            total_squares = lax.fori_loop(0, rows // 16, body, total_squares)
-        norms[w] = jnp.full((8, 128), total_squares, jnp.float32)
+                v = v * v
+                for k in range(v.shape[1] // 128):
+                    sums = sums + v[:, k * 128 : (k + 1) * 128]
+                return sums
+
+            squares = lax.fori_loop(0, rows // 16, body, squares)
+        norms[w] = jnp.full((8, 128), jnp.sum(squares), jnp.float32)
         for k in range(1, 8):
             sends.start(None, lambda k=k: copy(norms.at[w], norms.at[w], n_s.at[k], n_r.at[w], (peer(k), x * 2 + c)))
         for k in range(1, 8):
@@ -1115,12 +1130,23 @@
             whole = whole + norms[k]
         norm_out[...] = jnp.sqrt(whole)
 
-    def looped(n, body, steps):
+    moves = {
+        "add_x": add_x, "add_y": add_y, "line": line, "owner": owner, "middle_x": middle_x, "arrived": arrived,
+        "grads": lambda p, zz: grads(p, zz, dupper), "attention_grads": lambda zz: attention_grads(zz),
+    }
+    small_moves = {("add_y", 1, 3): small_y, ("owner", 1): small_add}
+
+    def run(steps):
+        for name, *rest in steps:
+            moves[name](*rest)
+            small_moves.get((name, *rest), lambda: None)()
+
+    def looped(n, body, table):
         @pl.loop(0, n)
         def _(i):
             body(i)
-            for k in sorted(steps):
-                pl.when(i == k)(lambda k=k: [step() for step in steps[k]] and None)
+            for k in sorted(table):
+                pl.when(i == k)(lambda k=k: run(table[k]))
 
     bar = pltpu.get_barrier_semaphore()
     for to in [near, over, diag] + [(peer(k), x * 2 + c) for k in range(1, 8)]:
@@ -1136,57 +1162,31 @@
         upper_back(k)
     need(L_HID)
     transpose_into(hid_m)
+    need(L_UP, L_DTWO, L_NORMED, L_INV, L_ATTN, L_DVEC)
+    hidden_back()
     for k in range(4):
         dup_copy(k).wait_recv()
-    for zz in ORDER:
-        grads(1, zz, dupper)
-    need(L_UP, L_DTWO, L_NORMED, L_INV, L_ATTN, L_DVEC)
-    hidden_back()
     need(L_QUERY, L_KV)
-    P = functools.partial
-    looped(seqs * 6, attend_back, {2: [P(add_x, 0, 3)], 5: [P(add_x, 0, 0)], 8: [P(add_x, 0, 2)], 11: [P(add_x, 0, 1)]})
+    looped(seqs * 6, attend_back, BESIDE_ATTENTION)
     swap(dquery, 1)
     small_start()
-    need(L_TOKENS, L_ROWS, L_MIXED)
+    need(L_TOKENS, L_ROWS, L_MIXED, L_PICK)
     key_value_grads()
+    small_x()
+    run(BESIDE_KEYS)
     for make in swaps:
         make().wait_recv()
     attention_sides()
-    for zz in ORDER:
-        attention_grads(zz)
     masked_tokens()
     tile = total // 256
-    looped(tile, tokens_back, {0: [P(add_y, 0, 3), small_x], 1: [P(add_y, 0, 0)], 2: [P(add_y, 0, 2)], 3: [P(add_y, 0, 1), small_y]})
+    looped(tile, tokens_back, BESIDE_TOKENS)
     for i in range(tile - 2, tile):
         token_store(i).wait()
     tile_load(0).start()
-    looped(tile * 4, feed_forward, {
-        0: [P(add_x, 1, 3), P(add_x, 1, 0)],
-        1: [P(line, 0, 0), small_add],
-        2: [P(add_x, 1, 2), P(add_x, 1, 1), P(line, 0, 1)],
-        3: [P(line, 0, 2), small_line],
-        4: [P(add_y, 1, 3), P(owner, 0)],
-        5: [P(add_y, 1, 0)],
-        6: [P(add_y, 1, 2), P(add_x, 2, 3)],
-        7: [P(add_y, 1, 1), P(add_x, 2, 0)],
-        8: [P(line, 1, 0), P(add_x, 2, 2)],
-        9: [P(line, 1, 1), P(add_x, 2, 1)],
-        10: [P(line, 1, 2), P(middle_x, 0)],
-        11: [P(owner, 1)],
-        12: [P(add_y, 2, 3)],
-        13: [P(add_y, 2, 0)],
-        14: [P(middle_x, 1)],
-        15: [P(add_y, 2, 2)],
-    })
-    add_y(2, 1)
-    for t in range(3):
-        line(2, t)
-    owner(2)
-    middle_x(2)
+    looped(tile * 4, feed_forward, BESIDE_FEED_FORWARD)
+    run(LAST)
     for i in range(tile - 2, tile):
         layer_store(i).wait()
-    for p in range(3):
-        arrived(p)
     square_sum()
     sends.finish()
     for make in swaps:
@@ -1195,12 +1195,11 @@
         dup_copy(k).wait_send()
 
 
-def backward(attn, up, down, vec, bias, kv, hidden, query_m, rows_m, mixed_m, hid_m, act_m, slope, dtwo, dlow, normed, inverse, dvec, tokens, spots):
+def backward(attn, up, down, vec, bias, kv, hidden, query_m, rows_m, mixed_m, hid_m, act_m, slope, dtwo, dlow, normed, inverse, dvec, pick_t, tokens):
     total, width = hidden.shape
     cols = up.shape[1]
     rows = width // 8
-    seqs, padded = spots.shape
-    length = total // seqs
+    seqs, length, padded = pick_t.shape
     count = seqs * padded
     shape = jax.ShapeDtypeStruct
     f = jnp.float32
@@ -1208,24 +1207,24 @@
     vm = pl.BlockSpec(memory_space=pltpu.VMEM)
     dma = pltpu.SemaphoreType.DMA
     v = pltpu.VMEM
-    inputs = (attn, up, down, vec, bias, kv, hidden, query_m, rows_m, mixed_m, hid_m, act_m, slope, dtwo, dlow, normed, inverse, dvec, tokens, spots)
+    inputs = (attn, up, down, vec, bias, kv, hidden, query_m, rows_m, mixed_m, hid_m, act_m, slope, dtwo, dlow, normed, inverse, dvec, pick_t, tokens)
 
     def like(a):
         return v(a.shape, a.dtype)
 
     one = (16, 128)
-    scratch = [like(a) for a in (attn, up, down, kv, query_m, rows_m, mixed_m, hid_m, act_m, slope, dtwo, dlow, normed, inverse, dvec, tokens)]
+    scratch = [like(a) for a in (attn, up, down, kv, query_m, rows_m, mixed_m, hid_m, act_m, slope, dtwo, dlow, normed, inverse, dvec, pick_t, tokens)]
     scratch += [
         v((2, width, count), LOW), v((2, count, width), LOW), v((2, count, cols), LOW), v((1, cols), f), v((count, width), f), v((count, width), f),
         v((2, count, width), LOW), v((count, width), LOW), v((2, count, width), LOW), v((2, total, width), LOW), v((width, M), LOW), v((width, total), LOW),
         v((2, 256, width), f), v((256, width), f), v((2, 256, width), LOW),
         v((3, width, M), LOW), v((3, width, E), LOW), v((3, 4, rows, M), LOW), v((3, 5, rows, M), LOW), v((3, rows, M), LOW),
-        v((8,) + one, f), v((8,) + one, f), v((8,) + one, f), v((8,) + one, f), v((4,) + one, f), v((4,) + one, f), v((4,) + one, f), v((8, 8, 128), f),
-        dma((16,)), dma((2,)), dma((4,)), dma((2,)), dma((2,)), dma((4,)), dma((4,)), dma((4,)), dma((4,)), dma((3, 4)), dma((3, 4)), dma((3, 4)), dma((3, 4)),
-        dma((2, 3, 4)), dma((2, 3, 4)), dma((3,)), dma((3,)), dma((3, 3)), dma((3, 3)), dma((14,)), dma((14,)), dma((8,)), dma((8,)),
+        v((8,) + one, f), v((8,) + one, f), v((8,) + one, f), v((8,) + one, f), v((8,) + one, f), v((8, 8, 128), f),
+        dma((17,)), dma((2,)), dma((4,)), dma((2,)), dma((2,)), dma((4,)), dma((4,)), dma((4,)), dma((4,)), dma((3, 4)), dma((3, 4)), dma((3, 4)), dma((3, 4)),
+        dma((2, 3, 4)), dma((2, 3, 4)), dma((3,)), dma((3,)), dma((3, 3)), dma((3, 3)), dma((9,)), dma((2,)), dma((8,)), dma((8,)), dma((8,)),
     ]
     specs = [anywhere] * len(inputs)
-    specs[3] = specs[4] = specs[19] = vm
+    specs[3] = specs[4] = vm
     return pl.pallas_call(
         functools.partial(backward_kernel, rows, seqs, length, padded),
         out_shape=(shape((total, width), LOW), shape((total, width), f), shape((3, rows, cols), LOW), shape(one, f), shape((8, 128), f)),
@@ -1236,6 +1235,102 @@
     )(*inputs)
 
 
+def adam_kernel(layer, dtokens, norm, own, small, *refs):
+    weights, firsts, seconds = refs[0:6], refs[6:12], refs[12:18]
+    outs = refs[18:36]
+    layer_o, dtokens_o, norm_o, layer_v, dtokens_v, sem = refs[36:]
+    step_id = pl.program_id(0)
+    copies_in = [pltpu.make_async_copy(layer, layer_v, sem.at[0]), pltpu.make_async_copy(dtokens, dtokens_v, sem.at[1])]
+    copies_out = [pltpu.make_async_copy(layer_v, layer_o, sem.at[2]), pltpu.make_async_copy(dtokens_v, dtokens_o, sem.at[3])]
+
+    @pl.when(step_id == 0)
+    def _():
+        for copy in copies_in:
+            copy.start()
+        norm_o[0, 0] = jnp.max(norm[...])
+
+    @pl.when(step_id == 2)
+    def _():
+        for first, then in zip(copies_in, copies_out):
+            first.wait()
+            then.start()
+
+    factor = CLIP_LIMIT / jnp.maximum(norm[0:1, 0:1], CLIP_LIMIT)
+
+    def step(k, where, grad, decay, rate):
+        grad = grad * factor.reshape((1,) * grad.ndim)
+        weight = weights[k][where]
+        first = BETA_ONE * firsts[k][where] + (1.0 - BETA_ONE) * grad
+        second = BETA_TWO * seconds[k][where] + (1.0 - BETA_TWO) * grad * grad
+        mean_hat = first * (1.0 / (1.0 - BETA_ONE**STEP))
+        square_hat = second * (1.0 / (1.0 - BETA_TWO**STEP))
+        outs[3 * k][where] = weight - rate * (mean_hat / (jnp.sqrt(square_hat) + ADAM_EPS) + decay * weight)
+        outs[3 * k + 1][where] = first
+        outs[3 * k + 2][where] = second
+
+    width = weights[1].shape[1]
+    for k in range(3):
+        step(0, (k,), f32(own[2, :, pl.ds(k * width, width)]), DECAY_RATE, LEARN_RATE)
+    everything = (slice(None), slice(None))
+    step(1, everything, f32(own[2, :, pl.ds(3 * width, width)]), DECAY_RATE, OUTPUT_RATE)
+    for k in range(4):
+        cols = (slice(None), pl.ds(k * width, width))
+        step(2, cols, f32(own[1, :, pl.ds(k * width, width)]), DECAY_RATE, LEARN_RATE)
+        step(3, cols, f32(own[0, :, pl.ds(k * width, width)]), DECAY_RATE, LEARN_RATE)
+
+    @pl.when(step_id == pl.num_programs(0) - 1)
+    def _():
+        for copy in copies_out:
+            copy.wait()
+
+    @pl.when(step_id == 0)
+    def _():
+        lanes = weights[4].shape[1]
+        step(4, everything, small[0:8, 0:lanes], 0.0, VECTOR_RATE)
+        step(5, everything, small[8:11, :], 0.0, BIAS_RATE)
+
+
+def adam(layer, dtokens, norm, own, small, weights, moments):
+    def turn(values):
+        a, b, c, d, e, g = values
+        return a, b.T, c, d.T, e, g.reshape(3, 128)
+
+    arrays = turn(weights) + turn([m[0] for m in moments]) + turn([m[1] for m in moments])
+    rows, cols = arrays[2].shape
+    width = cols // 4
+    slab = 16
+    anywhere = pl.BlockSpec(memory_space=pl.ANY)
+    specs = [
+        pl.BlockSpec((3, slab, width), lambda i: (0, i, 0)),
+        pl.BlockSpec((slab, width), lambda i: (i, 0)),
+        pl.BlockSpec((slab, cols), lambda i: (i, 0)),
+        pl.BlockSpec((slab, cols), lambda i: (i, 0)),
+        pl.BlockSpec(arrays[4].shape, lambda i: (0, 0)),
+        pl.BlockSpec(arrays[5].shape, lambda i: (0, 0)),
+    ]
+    outs = pl.pallas_call(
+        adam_kernel,
+        grid=(rows // slab,),
+        out_shape=tuple(jax.ShapeDtypeStruct(a.shape, a.dtype) for a in arrays[:6] for _ in range(3))
+        + (jax.ShapeDtypeStruct(layer.shape, layer.dtype), jax.ShapeDtypeStruct(dtokens.shape, dtokens.dtype), jax.ShapeDtypeStruct((1, 1), jnp.float32)),
+        in_specs=[
+            anywhere,
+            anywhere,
+            pl.BlockSpec(norm.shape, lambda i: (0, 0)),
+            pl.BlockSpec((3, slab, cols), lambda i: (0, i, 0)),
+            pl.BlockSpec(small.shape, lambda i: (0, 0)),
+        ] + specs * 3,
+        out_specs=tuple(s for s in specs for _ in range(3)) + (anywhere, anywhere, pl.BlockSpec(memory_space=pltpu.SMEM)),
+        scratch_shapes=[pltpu.VMEM(layer.shape, layer.dtype), pltpu.VMEM(dtokens.shape, dtokens.dtype), pltpu.SemaphoreType.DMA((4,))],
+        compiler_params=pltpu.CompilerParams(vmem_limit_bytes=64 * 2**20 - 2**16),
+    )(layer, dtokens, norm, own, small, *arrays)
+
+    def back(k, v):
+        return v.T if k in (1, 3) else v.reshape(-1) if k == 5 else v
+
+    return (outs[18], outs[19], outs[20].reshape(())) + tuple(back(i // 3, v) for i, v in enumerate(outs[:18]))
+
+
 def masks(mask_place, mask_count, gradient, length):
     seqs, slots = mask_place.shape
     padded = -(-slots // 16) * 16
@@ -1244,7 +1339,7 @@
     pick = (spots[:, :, None] == jnp.arange(length)[None, None, :]) & live[:, :, None]
     gradient = jnp.pad(gradient, ((0, 0), (0, padded - slots), (0, 0)))
     gradient = jnp.where(live[:, :, None], gradient, jnp.zeros_like(gradient))
-    return pick, jnp.where(live, spots, -1), gradient.reshape(seqs * padded, -1)
+    return pick, gradient.reshape(seqs * padded, -1)
 
 
 def update(weights, moments, grads, grad_norm):
@@ -1267,14 +1362,10 @@
     return attn.astype(jnp.bfloat16), up.astype(jnp.bfloat16), down.T.astype(jnp.bfloat16)
 
 
-def small_pack(vectors, bias):
-    rows = vectors.shape[1]
-    return jnp.concatenate([jnp.pad(vectors, ((0, 0), (0, 128 - rows))), bias.reshape(-1, 128), jnp.zeros((5, 128))])
-
-
-def plain(tokens, pick, spots, gradient, weights):
+def plain(tokens, mask_place, mask_count, gradient, weights, moments):
     low = jnp.bfloat16
     seqs, length, width = tokens.shape
+    pick, gradient = masks(mask_place, mask_count, gradient, length)
     padded = pick.shape[1]
     flat = tokens.reshape(seqs * length, width)
     attn_w, up_w, down_w = (lax.all_gather(v, "wide", axis=0, tiled=True) for v in pack(*weights[:4]))
@@ -1343,7 +1434,7 @@
 
     grads = (owned(dattn, 0), owned(dup, 0), owned(ddown, 0), owned(dvectors, 1), owned(dup_bias, 0))
     grad_norm = jnp.sqrt(lax.psum(sum(jnp.sum(v * v) for v in grads), "wide"))
-    return layer_out, dtokens, grads, grad_norm
+    return (layer_out, dtokens, grad_norm) + update(weights, moments, natural(*grads), grad_norm)
 
 
 def spread(pick, rows):
@@ -1357,25 +1448,20 @@
     ).reshape(seqs * length, -1)
 
 
-def tailored(tokens, pick, spots, gradient, weights):
-    low = jnp.bfloat16
+def tailored(tokens, mask_place, mask_count, gradient, weights, moments):
     seqs, length, width = tokens.shape
     flat = tokens.reshape(seqs * length, width)
-    saved = forward(*pack(*weights[:4]), small_pack(*weights[4:]).astype(low), flat, pick.astype(low), gradient)
-    layer_out, dtokens, own, small, grad_norm = backward(*saved, flat, spots)
-    own = own.astype(jnp.float32)
-    rows = own.shape[1]
-    return layer_out, dtokens, (own[2], own[1], own[0], small[:8, :rows], small[8:11].reshape(-1)), grad_norm[0, 0]
+    saved = forward(*weights, flat, mask_place, mask_count, gradient)
+    layer_out, dtokens, own, small, grad_norm = backward(*saved, flat)
+    return adam(layer_out, dtokens, grad_norm, own, small, weights, moments)
 
 
 def shards(body, tokens, mask_place, mask_count, masked_output_gradient, *parameters):
     seqs, length, width = tokens.shape
     weights = parameters[0::3]
     moments = tuple(zip(parameters[1::3], parameters[2::3]))
-    pick, spots, gradient = masks(mask_place, mask_count, masked_output_gradient, length)
-    layer_out, dtokens, grads, grad_norm = body(tokens, pick, spots, gradient, weights)
-    layer_out, dtokens = (v.reshape(seqs, length, width) for v in (layer_out, dtokens))
-    return (layer_out, dtokens, grad_norm) + update(weights, moments, natural(*grads), grad_norm)
+    layer_out, dtokens, *rest = body(tokens, mask_place, mask_count, masked_output_gradient, weights, moments)
+    return (layer_out.reshape(seqs, length, width), dtokens.reshape(seqs, length, width), *rest)
 
 
 def solution(mesh):

time: 268 us -> 205 us (0.76)
  Pallas kernels: 229 us -> 199 us
  other arithmetic: 22.3 us -> 0 us
  local copies, waits for them, and re-layouts: 10.6 us -> 1.66 us
    pallas_call x1, Pallas kernels: 148 us -> 106 us  [backward(): pl.pallas_call(functools.partial(backward_kernel, rows, seqs, length, pad...]
    pallas_call x0 -> x1, Pallas kernels: none -> 13 us  [adam(): pl.pallas_call(adam_kernel, grid=(rows // slab,), out_shape=tuple((jax.Sh...]
    sub x6 -> x0, other arithmetic: 10.5 us -> none  [adam_step(): weight - rate * (mean_hat / (jnp.sqrt(square_hat) + ADAM_EPS) + decay * w...]
    unnamed x36 -> x1, local copies, waits for them, and re-layouts: 8.35 us -> 1.66 us
    convert_element_type x4 -> x0, other arithmetic: 4.44 us -> none  [the longest x1 1.88 us: tailored(): own = own.astype(jnp.float32)]
where the time goes in v1:
time: 205 us; the launch traced here: 202 us
  Pallas kernels  199 us (97%)
    pallas_call x1, Pallas kernels, backward(): pl.pallas_call(functools.partial(backward_kernel, rows, seqs, length, pad...  106 us
    pallas_call x1, Pallas kernels, forward(): pl.pallas_call(functools.partial(forward_kernel, rows, seqs, length, padd...  80.7 us
    pallas_call x1, Pallas kernels, adam(): pl.pallas_call(adam_kernel, grid=(rows // slab,), out_shape=tuple((jax.Sh...  13 us

profile of v1, /device:TPU:0, one launch (start us, length us, event | category | flops | bytes accessed | tf_op | source)
XLA Modules:
  0.0 202.0 jit_solution(5837570743965066059)
XLA Ops:
  0.7 1.7 copy.43.grad_m
  2.3 80.7 %shard_map.373 = (bf16[768,3072]{1,0:T(8,128)(2,1)}, bf16[768,3072]{1,0:T(8,128)(2,1)}, bf16[768,3072]{1,0:T(8,128)(2,1)}, f32[8,768]{1,0:T(8,128)}, f32[1,3072]...) custom-call(f32[3,96,768]{2,1,0:T(8,128)} %refs_0_.1, ...), custom_call_target="tpu_custom_call" | custom-call | tf_op jit(solution)/shard_map/pallas_call | solution.py:681
  83.1 105.6 %shard_map.374 = (bf16[1024,768]{1,0:T(8,128)(2,1)}, f32[1024,768]{1,0:T(8,128)}, bf16[3,96,3072]{2,1,0:T(8,128)(2,1)}, f32[16,128]{1,0:T(8,128)}, f32[8,128]{1,0:T(8,128)}) custom-call(bf16[768,3072]{1,0:T(8,128)(2,1)} %get-tuple-element.66.attn_h, bf16[768,3072]{1,0:T(8,128)(2,1)} %get-tuple-element.67.up_h, bf16[768,3072]{1,0:T(8,128)(2,1)} %get-tuple-element.68.down_h, ...), custom_call_target="tpu_custom_call" | custom-call | tf_op jit(solution)/shard_map/pallas_call | solution.py:1228
  188.7 13.0 %shard_map.375 = (f32[3,96,768]{2,1,0:T(8,128)}, f32[3,96,768]{2,1,0:T(8,128)}, f32[3,96,768]{2,1,0:T(8,128)}, f32[96,768]{1,0:T(8,128)}, f32[96,768]{1,0:T(8,12...) custom-call(bf16[1024,768]{1,0:T(8,128)(2,1)} %get-tuple-element.85., ...), custom_call_target="tpu_custom_call" | custom-call | tf_op jit(solution)/shard_map/pallas_call | solution.py:1311

commit v2 on v1

--- a/solution.py
+++ b/solution.py
@@ -314,6 +314,21 @@
     return (weight_new, first_new, second_new)
 
 
+GATHER_ORDER = (
+    ("z_step", 0, 1), ("y_step", 0, 0), ("z_step", 0, 2), ("y_step", 0, 1), ("z_step", 0, 3), ("own", 1),
+    ("x_step", 0, 1), ("y_step", 0, 2), ("y_step", 0, 3), ("x_step", 0, 0), ("z_step", 1, 1), ("vectors_in",),
+    ("x_step", 0, 2), ("x_step", 0, 3), ("y_step", 1, 0), ("z_step", 1, 2), ("last", 0), ("project", 0),
+    ("project", 1), ("project", 2), ("own", 2), ("z_step", 1, 3), ("project", 3), ("x_step", 1, 0),
+    ("attend", 0), ("y_step", 1, 1), ("attend", 1), ("attend", 2), ("z_step", 2, 1), ("attend", 3),
+    ("y_step", 1, 2), ("attend", 4), ("attend", 5), ("attend", 6), ("x_step", 1, 1), ("y_step", 1, 3),
+    ("attend", 7), ("z_step", 2, 2), ("y_step", 2, 0), ("attend", 8), ("attend", 9), ("attend", 10),
+    ("x_step", 1, 2), ("attend", 11), ("x_step", 1, 3), ("z_step", 2, 3), ("middle", 0), ("middle", 1),
+    ("y_step", 2, 1), ("middle", 2), ("middle", 3), ("masked",), ("x_step", 2, 1), ("x_step", 2, 0),
+    ("y_step", 2, 2), ("save_hidden",), ("last", 1), ("upper", 0), ("y_step", 2, 3), ("upper", 1),
+    ("x_step", 2, 2), ("upper", 2), ("x_step", 2, 3), ("upper", 3), ("last", 2),
+)
+
+
 def dot(a, b, dims):
     return lax.dot_general(a, b, (dims, ((), ())), preferred_element_type=jnp.float32)
 
@@ -491,10 +506,11 @@
             kept = jnp.logical_and(row == slot, slot < count_m[s]).astype(jnp.float32).astype(LOW)
             pick[s] = dot(same, hit, NT).astype(LOW)
             pick_t[s] = dot(hit, same, NT).astype(LOW)
-            grad[pl.ds(s * padded, padded), :] = dot(kept, grad_m[s], NN)
+            grad[pl.ds(s * padded, padded), :] = dot(kept, f32(grad_m[...])[:, s, :].astype(LOW), NN)
         keep(pick_t, pick_o, 18)
 
     def vectors_in():
+        loads[4].wait()
         for k in range(1, 8):
             small_copy(k, peer(k)).wait_recv()
         at = lax.broadcasted_iota(jnp.int32, (128, width), 0)
@@ -613,36 +629,13 @@
         keep(hidden, hidden_o, 9)
         keep(qkv.at[pl.ds(1, 2)], kv_o, 10)
 
-    Z, Y, X, L = z_step, y_step, x_step, last
-    head = (
-        (Z, 0, 1), (Y, 0, 0), (Z, 0, 2), (Y, 0, 1), (X, 0, 0), (Z, 0, 3), (own, 1), (Y, 0, 2), (X, 0, 1), (vectors_in,), (Y, 0, 3), (X, 0, 2), (Z, 1, 1), (X, 0, 3), (L, 0),
-    )
-    links = (
-        (Y, 1, 0), (Z, 1, 2), (Y, 1, 1), (X, 1, 0), (Z, 1, 3), (own, 2), (Y, 1, 2), (X, 1, 1), (Y, 1, 3), (X, 1, 2), (Z, 2, 1), (X, 1, 3), (L, 1), (Y, 2, 0), (Z, 2, 2), (Y, 2, 1), (X, 2, 0), (Z, 2, 3),
-    )
-    ends = ((Y, 2, 2), (X, 2, 1), (Y, 2, 3), (X, 2, 2), (X, 2, 3))
-    work = [functools.partial(project, i) for i in range(4)]
-    work += [functools.partial(attend, s, j) for s in range(seqs) for j in range(width // 128)]
-    work += [functools.partial(middle, i) for i in range(4)]
-    work += [masked_rows, save_hidden]
-    for step, *rest in head:
-        step(*rest)
-    loads[4].wait()
-    done = 0
-    for k, (step, *rest) in enumerate(links):
-        upto = len(work) * (k + 1) // len(links)
-        for piece in work[done:upto]:
-            piece()
-        done = upto
-        step(*rest)
-    for k in range(4):
-        upper(k)
-        step, *rest = ends[k]
-        step(*rest)
-    step, *rest = ends[4]
-    step(*rest)
+    steps = {
+        "z_step": z_step, "y_step": y_step, "x_step": x_step, "own": own, "last": last, "vectors_in": vectors_in, "project": project,
+        "attend": lambda i: attend(i // (width // 128), i % (width // 128)), "middle": middle, "masked": masked_rows, "save_hidden": save_hidden, "upper": upper,
+    }
+    for name, *rest in GATHER_ORDER:
+        steps[name](*rest)
     after_upper()
-    last(2)
     lower()
     keep(vec, vec_o, 11)
     keep(bias, bias_o, 12)
@@ -659,7 +652,7 @@
 
 def forward(qkv, out, up, down, vectors, up_bias, tokens, place_m, count_m, grad_m):
     rows, cols = up.shape
-    out, down = out.T, down.T
+    out, down, grad_m = out.T, down.T, jnp.swapaxes(grad_m, 0, 1)
     total, width = tokens.shape
     seqs, slots = place_m.shape
     length = total // seqs
@@ -699,12 +692,12 @@
 E = 768
 M = 1536
 SLAB = 32
-ORDER = (3, 0, 2, 1)
-BESIDE_ATTENTION = {1: (("add_x", 0, 3), ("grads", 1, 3),), 3: (("grads", 1, 0),), 4: (("add_x", 0, 0),), 5: (("grads", 1, 2),), 7: (("add_x", 0, 2), ("grads", 1, 1),), 10: (("add_x", 0, 1),)}
-BESIDE_KEYS = (("add_x", 1, 3), ("add_y", 0, 3), ("add_x", 1, 0),)
-BESIDE_TOKENS = {0: (("add_x", 1, 2), ("add_y", 0, 0), ("line", 0, 0),), 1: (("attention_grads", 3),), 2: (("add_x", 1, 1),), 3: (("add_y", 0, 2), ("attention_grads", 0),)}
-BESIDE_FEED_FORWARD = {0: (("add_x", 2, 3),), 1: (("attention_grads", 2),), 2: (("add_x", 2, 0), ("add_y", 0, 1), ("line", 0, 1),), 3: (("add_y", 1, 3), ("attention_grads", 1),), 4: (("add_x", 2, 2), ("add_y", 1, 0), ("line", 1, 0), ("add_y", 1, 2),), 6: (("line", 0, 2), ("add_x", 2, 1),), 8: (("add_y", 1, 1),), 9: (("line", 1, 1),), 12: (("add_y", 2, 3),), 13: (("owner", 0),)}
-LAST = (("add_y", 2, 0), ("line", 2, 0), ("line", 1, 2), ("add_y", 2, 2), ("add_y", 2, 1), ("owner", 1), ("line", 2, 1), ("line", 2, 2), ("middle_x", 0), ("owner", 2), ("arrived", 0), ("middle_x", 1), ("arrived", 1), ("middle_x", 2), ("arrived", 2),)
+ORDER = (0, 1, 2, 3)
+BESIDE_ATTENTION = {2: (("add_x", 0, 0), ("add_x", 0, 1),), 4: (("grads", 1, 0), ("grads", 1, 2), ("add_x", 0, 2),), 10: (("add_y", 0, 0), ("add_x", 0, 3),)}
+BESIDE_KEYS = (("line", 0, 0), ("grads", 1, 1), ("add_y", 0, 1), ("grads", 1, 3), ("add_x", 1, 0), ("line", 0, 1), ("add_x", 1, 1), ("add_y", 0, 2),)
+BESIDE_TOKENS = {2: (("attention_grads", 0), ("line", 0, 2),), 3: (("add_x", 1, 3), ("add_y", 0, 3),)}
+BESIDE_FEED_FORWARD = {2: (("add_y", 1, 0), ("line", 1, 0),), 3: (("attention_grads", 1),), 4: (("add_x", 1, 2),), 5: (("add_y", 1, 1), ("line", 1, 1),), 6: (("add_x", 2, 0), ("add_x", 2, 1),), 7: (("owner", 0),), 9: (("add_y", 2, 0), ("line", 2, 0), ("add_y", 1, 2), ("attention_grads", 3), ("attention_grads", 2), ("line", 1, 2),), 12: (("add_y", 2, 1),), 13: (("line", 2, 1),), 14: (("add_x", 2, 3), ("add_y", 1, 3), ("add_x", 2, 2), ("owner", 1),)}
+LAST = (("add_y", 2, 3), ("add_y", 2, 2), ("line", 2, 2), ("middle_x", 0), ("middle_x", 1), ("owner", 2), ("arrived", 0), ("arrived", 1), ("middle_x", 2), ("arrived", 2),)
 
 
 def slabs(rows, body):
@@ -761,8 +754,15 @@
     def wait(cond, dst, rs):
         when(cond, lambda: copy(dst, dst, rs, rs, me).wait_recv())
 
-    def zrows(zz):
-        return pl.ds(zz * pair, pair)
+    def turn(k):
+        picks = ((3, 3, 0, 0), (2, 0, 3, 1), (1, 2, 1, 2), (0, 1, 2, 3))[k]
+        value = jnp.int32(picks[0])
+        for zv in range(1, 4):
+            value = jnp.where(z == zv, picks[zv], value)
+        return value
+
+    def zrows(k):
+        return pl.ds(pl.multiple_of(turn(k) * pair, pair), pair)
 
     def wrows(zz, yy):
         return pl.ds(pl.multiple_of((zz * 2 + yy) * rows, rows), rows)
@@ -772,8 +772,10 @@
         def _():
             wait(None, xb.at[p, zrows(zz)], x_r.at[p, zz])
 
+            base = turn(zz) * pair
+
             def one(i):
-                r = pl.ds(zz * pair + i, SLAB)
+                r = pl.ds(pl.multiple_of(base + i, SLAB), SLAB)
                 acc[p, r, pl.ds(0, E)] = (f32(acc[p, r, pl.ds(0, E)]) + f32(xb[p, r, :])).astype(LOW)
 
             slabs(pair, one)
@@ -785,7 +787,7 @@
 
     def push_y(cond, p, zz, wide):
         sends.start(cond, lambda: copy(
-            acc.at[p, wrows(zz, flip(y)), pl.ds(0, wide)], yr.at[p, zz, :, pl.ds(0, wide)], y_s.at[p, zz], y_r.at[p, zz], beside))
+            acc.at[p, wrows(turn(zz), flip(y)), pl.ds(0, wide)], yr.at[p, zz, :, pl.ds(0, wide)], y_s.at[p, zz], y_r.at[p, zz], beside))
 
     def add_into(cond, p, zz, buffer, slot, sem):
         for role, wide in ((edge, E), (mid, M)):
@@ -801,7 +803,7 @@
                 slabs(rows, one)
 
     def add_y(p, zz):
-        add_into(None, p, zz, yr, zz, y_r.at[p, zz])
+        add_into(None, p, turn(zz), yr, zz, y_r.at[p, zz])
 
     def z_push(cond, p, spot, k, to):
         for role, wide in ((edge, E), (mid, M)):
@@ -1002,8 +1004,10 @@
         def _():
             wait(None, part.at[zrows(zz)], sib_r.at[zz])
 
+            base = turn(zz) * pair
+
             def one(i):
-                r = pl.ds(zz * pair + i, SLAB)
+                r = pl.ds(pl.multiple_of(base + i, SLAB), SLAB)
                 acc[2, r, :] = (f32(acc[2, r, :]) + f32(part[r, :])).astype(LOW)
 
             slabs(pair, one)
@@ -1134,7 +1138,7 @@
         "add_x": add_x, "add_y": add_y, "line": line, "owner": owner, "middle_x": middle_x, "arrived": arrived,
         "grads": lambda p, zz: grads(p, zz, dupper), "attention_grads": lambda zz: attention_grads(zz),
     }
-    small_moves = {("add_y", 1, 3): small_y, ("owner", 1): small_add}
+    small_moves = {("add_y", 1, 0): small_y, ("owner", 1): small_add}
 
     def run(steps):
         for name, *rest in steps:

time: 205 us -> 190 us (0.927)
  Pallas kernels: 199 us -> 186 us
    pallas_call x1, Pallas kernels: 106 us -> 96.5 us  [backward(): pl.pallas_call(functools.partial(backward_kernel, rows, seqs, length, pad...]
    pallas_call x1, Pallas kernels: 80.7 us -> 76 us  [forward(): pl.pallas_call(functools.partial(forward_kernel, rows, seqs, length, padd...]
where the time goes in v2:
time: 190 us; the launch traced here: 186 us
  Pallas kernels  186 us (98%)
    pallas_call x1, Pallas kernels, backward(): pl.pallas_call(functools.partial(backward_kernel, rows, seqs, length, pad...  96.5 us
    pallas_call x1, Pallas kernels, forward(): pl.pallas_call(functools.partial(forward_kernel, rows, seqs, length, padd...  76 us
    pallas_call x1, Pallas kernels, adam(): pl.pallas_call(adam_kernel, grid=(rows // slab,), out_shape=tuple((jax.Sh...  13 us

profile of v2, /device:TPU:0, one launch (start us, length us, event | category | flops | bytes accessed | tf_op | source)
XLA Modules:
  0.0 186.5 jit_solution(236078902654263996)
XLA Ops:
  0.7 76.0 %shard_map.373 = (bf16[768,3072]{1,0:T(8,128)(2,1)}, bf16[768,3072]{1,0:T(8,128)(2,1)}, bf16[768,3072]{1,0:T(8,128)(2,1)}, f32[8,768]{1,0:T(8,128)}, f32[1,3072]...) custom-call(f32[3,96,768]{2,1,0:T(8,128)} %refs_0_.1, ...), custom_call_target="tpu_custom_call" | custom-call | tf_op jit(solution)/shard_map/pallas_call | solution.py:674
  76.6 96.5 %shard_map.374 = (bf16[1024,768]{1,0:T(8,128)(2,1)}, f32[1024,768]{1,0:T(8,128)}, bf16[3,96,3072]{2,1,0:T(8,128)(2,1)}, f32[16,128]{1,0:T(8,128)}, f32[8,128]{1,0:T(8,128)}) custom-call(bf16[768,3072]{1,0:T(8,128)(2,1)} %get-tuple-element.66.attn_h, bf16[768,3072]{1,0:T(8,128)(2,1)} %get-tuple-element.67.up_h, bf16[768,3072]{1,0:T(8,128)(2,1)} %get-tuple-element.68.down_h, ...), custom_call_target="tpu_custom_call" | custom-call | tf_op jit(solution)/shard_map/pallas_call | solution.py:1232
  173.2 13.0 %shard_map.375 = (f32[3,96,768]{2,1,0:T(8,128)}, f32[3,96,768]{2,1,0:T(8,128)}, f32[3,96,768]{2,1,0:T(8,128)}, f32[96,768]{1,0:T(8,128)}, f32[96,768]{1,0:T(8,12...) custom-call(bf16[1024,768]{1,0:T(8,128)(2,1)} %get-tuple-element.85., ...), custom_call_target="tpu_custom_call" | custom-call | tf_op jit(solution)/shard_map/pallas_call | solution.py:1315
